TPU v7x, 32 devices: a whole 2x2x4 slice. The times are simulated.
32 devices in a mesh: batch: 4 (over x, core), blk: 8 (over z, y).
Axes of the slice: x: 2, y: 2, z: 4, core: 2. Of those that a mesh axis runs over, the one named last changes fastest.
Arguments:
- tokens: bfloat16 [4, 1024, 1024], P('batch', 'blk'), may hold values from -6 to 6
- lengths: int32 [4], P('batch'), may hold values from 897 to 1024, as said below
- w_qkv: bfloat16 [1024, 3072], replicated, may hold values from -0.1875 to 0.1875
- qv_bias: float32 [2, 1024], replicated, may hold values from -1.5 to 1.5
- w_attn: bfloat16 [1024, 1024], replicated, may hold values from -3 to 3
- out_bias: float32 [2, 1024], replicated, may hold values from -1.5 to 1.5
- w_in: bfloat16 [1024, 4096], replicated, may hold values from -0.1875 to 0.1875
- in_bias: float32 [4096], replicated, may hold values from -1.5 to 1.5
- w_back: bfloat16 [4096, 1024], replicated, may hold values from -0.09375 to 0.09375
- norm_gain: float32 [2, 1024], replicated, may hold values from 0.1 to 1.9
- norm_shift: float32 [2, 1024], replicated, may hold values from -1.5 to 1.5
- cotangent: bfloat16 [4, 1024, 1024], P('batch', 'blk'), may hold values from -6 to 6
Outputs:
- mixed: bfloat16 [4, 1024, 1024], P('batch', 'blk')
- grad_tokens: bfloat16 [4, 1024, 1024], P('batch', 'blk')
- grad_qkv: float32 [1024, 3072], P('blk')
- grad_qv_bias: float32 [2, 1024], P(None, 'blk')
- grad_attn: float32 [1024, 1024], P('blk')
- grad_out_bias: float32 [2, 1024], P(None, 'blk')
- grad_in: float32 [1024, 4096], P('blk')
- grad_in_bias: float32 [4096], P('blk')
- grad_back: float32 [4096, 1024], P(None, 'blk')
- grad_gain: float32 [2, 1024], P(None, 'blk')
- grad_shift: float32 [2, 1024], P(None, 'blk')
Inputs may be any that keep to these rules, and one draw needn't show every extreme that they name: `lengths`: one sequence, drawn from the seed, has the full length 1024; every sequence has valid positions on the last device of its row.
All inputs are finite; a program needn't handle non-finite values.
Results may differ from a plain program's by a relative error of at most 0.025.
Values may be sent and summed in bfloat16 or wider, within the bound.
A program may use at most 448 MiB of HBM per device.

v0:
```python
import jax
import jax.numpy as jnp
from jax import lax
from jax.sharding import PartitionSpec as P

HEADS = 16


eps = 1e-12


def from_partner(x, axis, distance):
    return lax.ppermute(x, axis, [(i, i ^ 1 << distance) for i in range(lax.axis_size(axis))])


def normalize(values, gain, shift):
    centered = values - jnp.mean(values, axis=-1, keepdims=True)
    variance = jnp.mean(centered * centered, axis=-1, keepdims=True)
    return centered * lax.rsqrt(variance + eps) * gain + shift


def gelu_exact(values):
    return jax.nn.gelu(values, approximate=False)


def head_split(matrix, head_count):
    row_count, model_width = matrix.shape
    return matrix.reshape(row_count, head_count // 4, 4, model_width // head_count).transpose(
        1, 2, 0, 3
    )


def head_merge(stacked):
    group_count, group_size, row_count, head_size = stacked.shape
    return stacked.transpose(2, 0, 1, 3).reshape(row_count, group_count * group_size * head_size)


def core_forward(query_part, key_part, value_part, key_valid, scale):
    scores = (
        jnp.einsum("hqd,hkd->hqk", query_part, key_part, preferred_element_type=jnp.float32) * scale
    )
    masked = jnp.where(key_valid, scores, -1e30)
    row_max = jnp.max(masked, axis=-1, keepdims=True)
    exp_scores = jnp.where(key_valid, jnp.exp(masked - row_max), 0.0)
    row_total = jnp.sum(exp_scores, axis=-1, keepdims=True)
    prob_low = (exp_scores / row_total).astype(jnp.bfloat16)
    output = jnp.einsum("hqk,hkd->hqd", prob_low, value_part, preferred_element_type=jnp.float32)
    return (output, (row_max + jnp.log(row_total))[..., 0])


def core_backward(query_part, key_part, value_part, grad_part, log_part, key_valid, scale):
    scores = (
        jnp.einsum("hqd,hkd->hqk", query_part, key_part, preferred_element_type=jnp.float32) * scale
    )
    probs = jnp.where(key_valid, jnp.exp(scores - log_part[..., None]), 0.0)
    grad_probs = jnp.einsum(
        "hqd,hkd->hqk", grad_part, value_part, preferred_element_type=jnp.float32
    )
    inner_sum = jnp.sum(probs * grad_probs, axis=-1, keepdims=True)
    grad_scores = (probs * (grad_probs - inner_sum)).astype(jnp.bfloat16)
    grad_query = (
        jnp.einsum("hqk,hkd->hqd", grad_scores, key_part, preferred_element_type=jnp.float32)
        * scale
    )
    grad_key = (
        jnp.einsum("hqk,hqd->hkd", grad_scores, query_part, preferred_element_type=jnp.float32)
        * scale
    )
    grad_value = jnp.einsum(
        "hqk,hqd->hkd", probs.astype(jnp.bfloat16), grad_part, preferred_element_type=jnp.float32
    )
    return (grad_query, grad_key, grad_value)


def gather_group(kv_pair, position, bit_count):
    buffer_rows = kv_pair
    for step_bit in range(bit_count):
        received = from_partner(buffer_rows, "blk", step_bit)
        high_side = position >> step_bit & 1 == 1
        buffer_rows = jnp.where(
            high_side,
            jnp.concatenate([received, buffer_rows], 0),
            jnp.concatenate([buffer_rows, received], 0),
        )
    return buffer_rows


def spread_group(partials, position, bit_count):
    for step_bit in reversed(range(bit_count)):
        half_rows = partials.shape[0] // 2
        high_side = position >> step_bit & 1 == 1
        lower_part = partials[:half_rows]
        upper_part = partials[half_rows:]
        kept_part = jnp.where(high_side, upper_part, lower_part)
        sent_part = jnp.where(high_side, lower_part, upper_part)
        partials = kept_part + from_partner(sent_part.astype(jnp.bfloat16), "blk", step_bit).astype(
            sent_part.dtype
        )
    return partials


def attend_forward(queries, gathered, key_valid, head_count):
    model_width = queries.shape[1]
    scale = (model_width // head_count) ** (-0.5)
    query_heads = head_split(queries, head_count)
    key_heads = head_split(gathered[:, :model_width], head_count)
    value_heads = head_split(gathered[:, model_width:], head_count)

    def one_group(operands):
        query_part, key_part, value_part = operands
        return core_forward(query_part, key_part, value_part, key_valid, scale)

    outputs, log_sums = lax.map(one_group, (query_heads, key_heads, value_heads))
    return (head_merge(outputs), log_sums)


def attend_backward(queries, gathered, key_valid, log_sums, grad_attended, head_count):
    model_width = queries.shape[1]
    scale = (model_width // head_count) ** (-0.5)
    query_heads = head_split(queries, head_count)
    key_heads = head_split(gathered[:, :model_width], head_count)
    value_heads = head_split(gathered[:, model_width:], head_count)
    grad_heads = head_split(grad_attended, head_count)

    def one_group(operands):
        query_part, key_part, value_part, grad_part, log_part = operands
        return core_backward(
            query_part, key_part, value_part, grad_part, log_part, key_valid, scale
        )

    grad_query, grad_key, grad_value = lax.map(
        one_group, (query_heads, key_heads, value_heads, grad_heads, log_sums)
    )
    return (
        head_merge(grad_query),
        jnp.concatenate([head_merge(grad_key), head_merge(grad_value)], 1),
    )


def layer_forward(hidden, params, key_valid, position, bit_count, head_count):
    w_qkv, qv_bias, w_attn, out_bias, w_in, in_bias, w_back, norm_gain, norm_shift = params
    model_width = hidden.shape[1]
    hidden_low = hidden.astype(jnp.bfloat16)
    bias_row = jnp.concatenate([qv_bias[0], jnp.zeros_like(qv_bias[0]), qv_bias[1]])
    projected = (jnp.dot(hidden_low, w_qkv, preferred_element_type=jnp.float32) + bias_row).astype(
        jnp.bfloat16
    )
    gathered = gather_group(projected[:, model_width:], position, bit_count)
    attended, log_sums = attend_forward(projected[:, :model_width], gathered, key_valid, head_count)
    attended_low = attended.astype(jnp.bfloat16)
    first_sum = (
        hidden + jnp.dot(attended_low, w_attn, preferred_element_type=jnp.float32) + out_bias[0]
    )
    first_norm = normalize(first_sum, norm_gain[0], norm_shift[0])
    first_low = first_norm.astype(jnp.bfloat16)
    inner_pre = jnp.dot(first_low, w_in, preferred_element_type=jnp.float32) + in_bias
    activated = gelu_exact(inner_pre).astype(jnp.bfloat16)
    second_sum = (
        first_norm + jnp.dot(activated, w_back, preferred_element_type=jnp.float32) + out_bias[1]
    )
    output = normalize(second_sum, norm_gain[1], norm_shift[1])
    saved_state = (
        hidden_low,
        projected,
        gathered,
        log_sums,
        attended_low,
        first_sum,
        first_low,
        inner_pre,
        activated,
        second_sum,
    )
    return (output, saved_state)


def layer_backward(grad_output, saved_state, params, key_valid, position, bit_count, head_count):
    w_qkv, qv_bias, w_attn, out_bias, w_in, in_bias, w_back, norm_gain, norm_shift = params
    (
        hidden_low,
        projected,
        gathered,
        log_sums,
        attended_low,
        first_sum,
        first_low,
        inner_pre,
        activated,
        second_sum,
    ) = saved_state
    model_width = hidden_low.shape[1]
    unused_two, pull_two = jax.vjp(normalize, second_sum, norm_gain[1], norm_shift[1])
    grad_second, gain_two, shift_two = pull_two(grad_output)
    grad_branch_two = grad_second.astype(jnp.bfloat16)
    back_grad = jnp.einsum(
        "ra,rb->ab", activated, grad_branch_two, preferred_element_type=jnp.float32
    )
    bias_two = jnp.sum(grad_branch_two.astype(jnp.float32), axis=0)
    grad_act = jnp.dot(grad_branch_two, w_back.T, preferred_element_type=jnp.float32)
    unused_gelu, pull_gelu = jax.vjp(gelu_exact, inner_pre)
    grad_inner = pull_gelu(grad_act)[0].astype(jnp.bfloat16)
    in_grad = jnp.einsum("ra,rb->ab", first_low, grad_inner, preferred_element_type=jnp.float32)
    in_bias_grad = jnp.sum(grad_inner.astype(jnp.float32), axis=0)
    grad_first_norm = grad_second + jnp.dot(grad_inner, w_in.T, preferred_element_type=jnp.float32)
    unused_one, pull_one = jax.vjp(normalize, first_sum, norm_gain[0], norm_shift[0])
    grad_first, gain_one, shift_one = pull_one(grad_first_norm)
    grad_branch = grad_first.astype(jnp.bfloat16)
    attn_grad = jnp.einsum(
        "ra,rb->ab", attended_low, grad_branch, preferred_element_type=jnp.float32
    )
    bias_one = jnp.sum(grad_branch.astype(jnp.float32), axis=0)
    grad_attended = jnp.dot(grad_branch, w_attn.T, preferred_element_type=jnp.float32).astype(
        jnp.bfloat16
    )
    grad_query, grad_pairs = attend_backward(
        projected[:, :model_width], gathered, key_valid, log_sums, grad_attended, head_count
    )
    own_pairs = spread_group(grad_pairs, position, bit_count)
    grad_proj = jnp.concatenate([grad_query, own_pairs], 1).astype(jnp.bfloat16)
    qkv_grad = jnp.einsum("ra,rb->ab", hidden_low, grad_proj, preferred_element_type=jnp.float32)
    column_sums = jnp.sum(grad_proj.astype(jnp.float32), axis=0)
    qv_grad = jnp.stack([column_sums[:model_width], column_sums[2 * model_width :]])
    grad_hidden = grad_first + jnp.dot(grad_proj, w_qkv.T, preferred_element_type=jnp.float32)
    grad_list = (
        qkv_grad,
        qv_grad,
        attn_grad,
        jnp.stack([bias_one, bias_two]),
        in_grad,
        in_bias_grad,
        back_grad,
        jnp.stack([gain_one, gain_two]),
        jnp.stack([shift_one, shift_two]),
    )
    return (grad_hidden, grad_list)


def scatter_once(grad_list):
    (
        qkv_grad,
        qv_grad,
        attn_grad,
        bias_grad,
        in_grad,
        in_bias_grad,
        back_grad,
        gain_grad,
        shift_grad,
    ) = grad_list
    return (
        lax.psum_scatter(qkv_grad, "blk", scatter_dimension=0, tiled=True),
        lax.psum_scatter(qv_grad, "blk", scatter_dimension=1, tiled=True),
        lax.psum_scatter(attn_grad, "blk", scatter_dimension=0, tiled=True),
        lax.psum_scatter(bias_grad, "blk", scatter_dimension=1, tiled=True),
        lax.psum_scatter(in_grad, "blk", scatter_dimension=0, tiled=True),
        lax.psum_scatter(in_bias_grad, "blk", scatter_dimension=0, tiled=True),
        lax.psum_scatter(back_grad, "blk", scatter_dimension=1, tiled=True),
        lax.psum_scatter(gain_grad, "blk", scatter_dimension=1, tiled=True),
        lax.psum_scatter(shift_grad, "blk", scatter_dimension=1, tiled=True),
    )


def body(
    tokens,
    lengths,
    w_qkv,
    qv_bias,
    w_attn,
    out_bias,
    w_in,
    in_bias,
    w_back,
    norm_gain,
    norm_shift,
    cotangent,
):
    row_count = tokens.shape[1]
    head_count = HEADS
    cycle_size = lax.axis_size("blk")
    bit_count = cycle_size.bit_length() - 1
    position = lax.axis_index("blk")
    length = lengths[0]
    key_valid = jnp.arange(cycle_size * row_count) < length
    params = (w_qkv, qv_bias, w_attn, out_bias, w_in, in_bias, w_back, norm_gain, norm_shift)
    out_one, saved_one = layer_forward(
        tokens[0].astype(jnp.float32), params, key_valid, position, bit_count, head_count
    )
    out_two, saved_two = layer_forward(out_one, params, key_valid, position, bit_count, head_count)
    grad_hidden, grads_two = layer_backward(
        cotangent[0].astype(jnp.float32),
        saved_two,
        params,
        key_valid,
        position,
        bit_count,
        head_count,
    )
    grad_hidden, grads_one = layer_backward(
        grad_hidden, saved_one, params, key_valid, position, bit_count, head_count
    )
    shards = scatter_once(jax.tree.map(jnp.add, grads_two, grads_one))
    (
        qkv_part,
        qv_part,
        attn_part,
        bias_part,
        in_part,
        in_bias_part,
        back_part,
        gain_part,
        shift_part,
    ) = shards
    totals = (
        lax.psum(qkv_part.astype(jnp.bfloat16), "batch").astype(jnp.float32),
        lax.psum(qv_part.astype(jnp.bfloat16), "batch").astype(jnp.float32),
        lax.psum(attn_part.astype(jnp.bfloat16), "batch").astype(jnp.float32),
        lax.psum(bias_part.astype(jnp.bfloat16), "batch").astype(jnp.float32),
        lax.psum(in_part.astype(jnp.bfloat16), "batch").astype(jnp.float32),
        lax.psum(in_bias_part.astype(jnp.bfloat16), "batch").astype(jnp.float32),
        lax.psum(back_part.astype(jnp.bfloat16), "batch").astype(jnp.float32),
        lax.psum(gain_part.astype(jnp.bfloat16), "batch").astype(jnp.float32),
        lax.psum(shift_part.astype(jnp.bfloat16), "batch").astype(jnp.float32),
    )
    return (
        out_two.astype(jnp.bfloat16)[None],
        grad_hidden.astype(jnp.bfloat16)[None],
        totals[0],
        totals[1],
        totals[2],
        totals[3],
        totals[4],
        totals[5],
        totals[6],
        totals[7],
        totals[8],
    )


def solution(mesh):
    placed = (
        P("batch", "blk", None),
        P("batch"),
        P(),
        P(),
        P(),
        P(),
        P(),
        P(),
        P(),
        P(),
        P(),
        P("batch", "blk", None),
    )
    return jax.shard_map(
        body,
        mesh=mesh,
        in_specs=placed,
        out_specs=(
            P("batch", "blk", None),
            P("batch", "blk", None),
            P("blk", None),
            P(None, "blk"),
            P("blk", None),
            P(None, "blk"),
            P("blk", None),
            P("blk"),
            P(None, "blk"),
            P(None, "blk"),
            P(None, "blk"),
        ),
        check_vma=False,
    )
```

profile of v0, /device:TPU:1, one launch (start us, length us, event | category | flops | bytes accessed | tf_op | source)
XLA Modules:
  0.0 1924.1 jit_solution(2879120982853153745)
XLA Ops:
  8.1 3.9 fusion.96
  15.1 11.8 collective-permute-done
  30.0 22.3 %collective-permute-done.1 = bf16[256,2048]{1,0:T(8,128)(2,1)} collective-permute-done((bf16[256,2048]{1,0:T(8,128)(2,1)S(1)}, bf16[256,2048]{1,0:T(8,128)(2,1)}, u32[]{:S(2)}, u32[]{:S(2)}) %collective-permute-start.1) | collective-permute-done | bytes 1048608 | tf_op jit(solution)/shard_map/ppermute | solution.py:13
  52.3 3.8 maximum_select_fusion.2
  58.3 90.9 %collective-permute-done.2 = bf16[512,2048]{1,0:T(8,128)(2,1)} collective-permute-done((bf16[512,2048]{1,0:T(8,128)(2,1)}, bf16[512,2048]{1,0:T(8,128)(2,1)}, u32[]{:S(2)}, u32[]{:S(2)}) %collective-permute-start.2) | collective-permute-done | bytes 2097184 | tf_op jit(solution)/shard_map/ppermute | solution.py:13
  149.2 4.8 maximum_select_fusion
  156.5 4.0 copy.42
  160.5 3.9 copy.43
  164.5 19.2 while.56
  185.1 9.8 multiply_convert_fusion.3
  198.4 11.9 collective-permute-done.3
  212.0 21.2 %collective-permute-done.4 = bf16[256,2048]{1,0:T(8,128)(2,1)S(1)} collective-permute-done((bf16[256,2048]{1,0:T(8,128)(2,1)S(1)}, bf16[256,2048]{1,0:T(8,128)(2,1)S(1)}, u32[]{:S(2)}, u32[]{:S(2)}) %collective-permute-start.4) | collective-permute-done | bytes 1048608 | tf_op jit(solution)/shard_map/ppermute | solution.py:13
  235.6 4.0 collective-permute-start.5
  242.4 87.6 %collective-permute-done.5 = bf16[512,2048]{1,0:T(8,128)(2,1)} collective-permute-done((bf16[512,2048]{1,0:T(8,128)(2,1)}, bf16[512,2048]{1,0:T(8,128)(2,1)}, u32[]{:S(2)}, u32[]{:S(2)}) %collective-permute-start.5) | collective-permute-done | bytes 2097184 | tf_op jit(solution)/shard_map/ppermute | solution.py:13
  330.0 4.9 maximum_select_fusion.1
  337.3 4.0 copy.45
  341.3 3.9 copy.46
  346.0 22.1 %while.57 = (s32[]{:T(128)}, bf16[4,4,128,64]{2,3,1,0:T(8,128)(2,1)}, f32[4,4,128]{2,1,0:T(4,128)S(1)}, bf16[4,4,128,64]{2,3,1,0:T(8,128)(2,1)S(1)}, bf16[4,4,10...) while((s32[]{:T(128)}, ...), condition=%wide.region_11.12_spmd.clone, body=%wide.region_8.11_spmd.clone.sunk | while | flops 141558272 | bytes 9656477 | solution.py:113
  369.8 10.0 multiply_convert_fusion.2
  379.9 5.3 fusion.161
  388.0 6.3 convert_reduce_fusion.1
  409.5 32.6 %while.58 = (s32[]{:T(128)}, bf16[4,4,128,64]{2,3,1,0:T(8,128)(2,1)}, f32[4,4,1024,64]{2,3,1,0:T(8,128)}, f32[4,4,1024,64]{2,3,1,0:T(8,128)}, bf16[4,4,128,64]{2...) while((s32[]{:T(128)}, ...), condition=%wide.region_22.23_spmd.clone, body=%wide.region_20.22_spmd.clone.sunk | while | flops 340558336 | bytes 30295248 | solution.py:131
  442.1 4.0 select_convert_fusion.1
  446.2 91.5 %collective-permute-done.6 = bf16[512,2048]{0,1:T(8,128)(2,1)S(1)} collective-permute-done((bf16[512,2048]{0,1:T(8,128)(2,1)S(1)}, bf16[512,2048]{0,1:T(8,128)(2,1)S(1)}, u32[]{:S(2)}, u32[]{:S(2)}) %collective-permute-start.6) | collective-permute-done | bytes 2097184 | tf_op jit(solution)/shard_map/ppermute | solution.py:13
  540.0 22.3 %collective-permute-done.7 = bf16[256,2048]{0,1:T(8,128)(2,1)S(1)} collective-permute-done((bf16[256,2048]{0,1:T(8,128)(2,1)S(1)}, bf16[256,2048]{0,1:T(8,128)(2,1)S(1)}, u32[]{:S(2)}, u32[]{:S(2)}) %collective-permute-start.7) | collective-permute-done | bytes 1048608 | tf_op jit(solution)/shard_map/ppermute | solution.py:13
  566.9 6.2 collective-permute-done.8
  576.2 5.8 convert_reduce_fusion
  589.7 4.9 convolution_add_fusion.6
  600.5 35.5 %while.59 = (s32[]{:T(128)}, bf16[4,4,128,64]{2,3,1,0:T(8,128)(2,1)}, f32[4,4,1024,64]{2,3,1,0:T(8,128)}, f32[4,4,1024,64]{2,3,1,0:T(8,128)}, bf16[4,4,128,64]{2...) while((s32[]{:T(128)}, ...), condition=%wide.region_29.30_spmd.clone, body=%wide.region_27.29_spmd.clone.sunk | while | flops 340558336 | bytes 30295248 | solution.py:131
  635.9 4.1 select_convert_fusion
  640.1 6.3 collective-permute-start.9
  646.3 107.2 %collective-permute-done.9 = bf16[512,2048]{0,1:T(8,128)(2,1)S(1)} collective-permute-done((bf16[512,2048]{0,1:T(8,128)(2,1)S(1)}, bf16[512,2048]{0,1:T(8,128)(2,1)S(1)}, u32[]{:S(2)}, u32[]{:S(2)}) %collective-permute-start.9) | collective-permute-done | bytes 2097184 | tf_op jit(solution)/shard_map/ppermute | solution.py:13
  756.0 23.1 %collective-permute-done.10 = bf16[256,2048]{0,1:T(8,128)(2,1)S(1)} collective-permute-done((bf16[256,2048]{0,1:T(8,128)(2,1)S(1)}, bf16[256,2048]{0,1:T(8,128)(2,1)S(1)}, u32[]{:S(2)}, u32[]{:S(2)}) %collective-permute-start.10) | collective-permute-done | bytes 1048608 | tf_op jit(solution)/shard_map/ppermute | solution.py:13
  782.9 8.2 collective-permute-done.11
  792.0 6.3 bitcast_add_fusion
  802.2 9.1 convolution_add_fusion.1
  815.0 8.1 convolution_add_fusion
  831.2 178.5 %reduce-scatter.17.cloned.1.call-done = f32[128,3072]{1,0:T(8,128)} async-done(((f32[1024,3072]{1,0:T(8,128)}), f32[128,3072]{1,0:T(8,128)}) %reduce-scatter.17.cloned.1.call-update) | async-done | bytes 1572880 | tf_op jit(solution)/shard_map/reduce_scatter | solution.py:251
  1012.1 283.8 %reduce-scatter.21.cloned.1.call-done = f32[128,4096]{1,0:T(8,128)} async-done(((f32[1024,4096]{1,0:T(8,128)}), f32[128,4096]{1,0:T(8,128)}) %reduce-scatter.21.cloned.1.call-update) | async-done | bytes 2097168 | tf_op jit(solution)/shard_map/reduce_scatter | solution.py:255
  1298.6 282.6 %reduce-scatter.23.cloned.1.call-done = f32[4096,128]{1,0:T(8,128)} async-done(((f32[4096,1024]{1,0:T(8,128)}), f32[4096,128]{1,0:T(8,128)}) %reduce-scatter.23.cloned.1.call-update) | async-done | bytes 2097168 | tf_op jit(solution)/shard_map/reduce_scatter | solution.py:257
  1585.8 28.6 %all-reduce = bf16[4096]{0:T(1024)(128)(2,1)S(1)} all-reduce(f32[4096]{0:T(1024)S(1)} %add.328), channel_id=7, replica_groups=mesh['batch'=4,'blk'=8] {'blk'}, use_global_device_ids=true, to_apply=%region_48.49.clone | all-reduce | flops 4096 | bytes 24576
  1614.5 29.3 %reduce-scatter.27.cloned.1.call-done = f32[128,2]{1,0:T(8,128)} async-done(((f32[1024,2]{1,0:T(8,128)}), f32[128,2]{1,0:T(8,128)}) %reduce-scatter.27.cloned.1.call-update) | async-done | bytes 1040
  1644.7 63.3 %reduce-scatter.29.cloned.1.call-done = f32[128,2]{1,0:T(8,128)} async-done(((f32[1024,2]{1,0:T(8,128)}), f32[128,2]{1,0:T(8,128)}) %reduce-scatter.29.cloned.1.call-update) | async-done | bytes 1040
  1708.9 63.8 %reduce-scatter.31.cloned.1.call-done = f32[128,2]{1,0:T(8,128)} async-done(((f32[1024,2]{1,0:T(8,128)}), f32[128,2]{1,0:T(8,128)}) %reduce-scatter.31.cloned.1.call-update) | async-done | bytes 1040
  1773.6 5.7 fusion.115
  1779.3 57.7 %reduce-scatter.25.cloned.1.call-done = f32[128,2]{1,0:T(8,128)} async-done(((f32[1024,2]{1,0:T(8,128)}), f32[128,2]{1,0:T(8,128)}) %reduce-scatter.25.cloned.1.call-update) | async-done | bytes 1040
  1837.9 7.6 all-reduce.1
  1848.3 62.4 %all-reduce.5.cloned.1.call-done = (bf16[128,3072]{1,0:T(8,128)(2,1)}, bf16[128,1024]{1,0:T(8,128)(2,1)}, bf16[128,4096]{1,0:T(8,128)(2,1)}, bf16[4096,128]{1,0:T(8,128)(2,1)}) async-done(((bf16[128,3072]{1,0:T(8,128)(2,1)}, bf16[128,1024]{1,0:T(8,128)(2,1)}, bf16[128,4096]{1,0:T(8,128)(2,1)}, bf16[4096,128]{1,0:T(8,128)(2,1)}), (bf16[128,3072]{1,0:T(8,128)(2,1)}, bf16[128,1024]{1,0:T(8,128)(2,1)}, ...) | async-done | bytes 3145744 | tf_op jit(solution)/shard_map/psum | solution.py:314
  (469 shorter events, 222.0 us)
Async XLA Ops:
  7.2 177.1 %copy-start = (bf16[1024,1024]{1,0:T(8,128)(2,1)S(1)}, bf16[1024,1024]{1,0:T(8,128)(2,1)}, u32[]{:S(2)}) copy-start(bf16[1024,1024]{1,0:T(8,128)(2,1)} %param.24) | copy-start | bytes 6291460
  7.2 822.2 %reduce-scatter.19.cloned.1.call-start = ((), (), s32[]{:S(2)}) async-start(), calls=%async_computation.9 | async-start | bytes 4718592 | tf_op jit(solution)/shard_map/reduce_scatter | solution.py:253
  12.9 13.9 collective-permute-start
  28.8 23.6 %collective-permute-start.1 = (bf16[256,2048]{1,0:T(8,128)(2,1)S(1)}, bf16[256,2048]{1,0:T(8,128)(2,1)}, u32[]{:S(2)}, u32[]{:S(2)}) collective-permute-start(bf16[256,2048]{1,0:T(8,128)(2,1)S(1)} %maximum_select_fusion.4), channel_id=1, source_target_pairs={{0,2},{1,3},{2,0},{3,1},{4,6},{5,7},{6,4},{7,5},{8,10},{9,11},{10,... | collective-permute-start | bytes 3145736 | tf_op jit(solution)/shard_map/ppermute | solution.py:13
  30.0 28.0 %slice-start.14 = ((bf16[128,3072]{1,0:T(8,128)(2,1)}), bf16[128,1024]{1,0:T(8,128)(2,1)S(1)}, s32[]{:S(2)}) async-start(bf16[128,3072]{1,0:T(8,128)(2,1)} %copy-done.39), calls=%async_computation.31 | async-start | bytes 524288 | tf_op jit(solution)/shard_map/slice | solution.py:149
  30.0 28.2 %copy-start.64 = (f32[2,1024]{1,0:T(2,128)S(1)}, f32[2,1024]{1,0:T(2,128)}, u32[]{:S(2)}) copy-start(f32[2,1024]{1,0:T(2,128)} %param.25) | copy-start | bytes 24580
  30.0 28.2 %copy-start.65 = (f32[2,1024]{1,0:T(2,128)S(1)}, f32[2,1024]{1,0:T(2,128)}, u32[]{:S(2)}) copy-start(f32[2,1024]{1,0:T(2,128)} %param.30) | copy-start | bytes 24580
  30.0 28.3 %copy-start.66 = (f32[2,1024]{1,0:T(2,128)S(1)}, f32[2,1024]{1,0:T(2,128)}, u32[]{:S(2)}) copy-start(f32[2,1024]{1,0:T(2,128)} %param.29) | copy-start | bytes 24580
  56.2 93.1 %collective-permute-start.2 = (bf16[512,2048]{1,0:T(8,128)(2,1)}, bf16[512,2048]{1,0:T(8,128)(2,1)}, u32[]{:S(2)}, u32[]{:S(2)}) collective-permute-start(bf16[512,2048]{1,0:T(8,128)(2,1)} %maximum_select_fusion.2), channel_id=1, source_target_pairs={{0,4},{1,5},{2,6},{3,7},{4,0},{5,1},{6,2},{7,3},{8,12},{9,13},{10,... | collective-permute-start | bytes 6291464 | tf_op jit(solution)/shard_map/ppermute | solution.py:13
  164.5 19.8 %copy-start.37 = (bf16[1,128,1024]{2,1,0:T(8,128)(2,1)S(1)}, bf16[1,128,1024]{2,1,0:T(8,128)(2,1)}, u32[]{:S(2)}) copy-start(bf16[1,128,1024]{2,1,0:T(8,128)(2,1)} %param.20) | copy-start | bytes 786436
  183.7 11.3 copy-start.19
  183.7 11.3 copy-start.45
  184.3 10.7 slice-start.4
  184.3 12.4 slice-start
  185.1 9.9 slice-start.5
  185.1 11.6 slice-start.1
  197.9 12.4 copy-start.40
  197.9 12.3 collective-permute-start.3
  210.6 22.6 %collective-permute-start.4 = (bf16[256,2048]{1,0:T(8,128)(2,1)S(1)}, bf16[256,2048]{1,0:T(8,128)(2,1)S(1)}, u32[]{:S(2)}, u32[]{:S(2)}) collective-permute-start(bf16[256,2048]{1,0:T(8,128)(2,1)S(1)} %maximum_select_fusion.5), channel_id=1, source_target_pairs={{0,2},{1,3},{2,0},{3,1},{4,6},{5,7},{6,4},{7,5},{8,10},{9,11},{10,... | collective-permute-start | bytes 3145736 | tf_op jit(solution)/shard_map/ppermute | solution.py:13
  235.6 94.4 %collective-permute-start.5 = (bf16[512,2048]{1,0:T(8,128)(2,1)}, bf16[512,2048]{1,0:T(8,128)(2,1)}, u32[]{:S(2)}, u32[]{:S(2)}) collective-permute-start(bf16[512,2048]{1,0:T(8,128)(2,1)} %maximum_select_fusion.3), channel_id=1, source_target_pairs={{0,4},{1,5},{2,6},{3,7},{4,0},{5,1},{6,2},{7,3},{8,12},{9,13},{10,... | collective-permute-start | bytes 6291464 | tf_op jit(solution)/shard_map/ppermute | solution.py:13
  369.6 28.4 %copy-start.8 = (f32[128,1024]{1,0:T(8,128)}, f32[128,1024]{1,0:T(8,128)S(1)}, u32[]{:S(2)}) copy-start(f32[128,1024]{1,0:T(8,128)S(1)} %get-tuple-element.428) | copy-start | bytes 1572868
  379.9 14.5 slice-start.10
  442.1 95.6 %copy-start.6 = (f32[4,4,1024,64]{2,3,1,0:T(8,128)S(1)}, f32[4,4,1024,64]{2,3,1,0:T(8,128)}, u32[]{:S(2)}) copy-start(f32[4,4,1024,64]{2,3,1,0:T(8,128)} %get-tuple-element.199) | copy-start | bytes 12582916
  442.1 95.6 %copy-start.7 = (f32[4,4,1024,64]{2,3,1,0:T(8,128)S(1)}, f32[4,4,1024,64]{2,3,1,0:T(8,128)}, u32[]{:S(2)}) copy-start(f32[4,4,1024,64]{2,3,1,0:T(8,128)} %get-tuple-element.200) | copy-start | bytes 12582916
  446.2 91.6 %collective-permute-start.6 = (bf16[512,2048]{0,1:T(8,128)(2,1)S(1)}, bf16[512,2048]{0,1:T(8,128)(2,1)S(1)}, u32[]{:S(2)}, u32[]{:S(2)}) collective-permute-start(bf16[512,2048]{0,1:T(8,128)(2,1)S(1)} %select_convert_fusion.1), channel_id=1, source_target_pairs={{0,4},{1,5},{2,6},{3,7},{4,0},{5,1},{6,2},{7,3},{8,12},{9,13},{10,... | collective-permute-start | bytes 6291464 | tf_op jit(solution)/shard_map/ppermute | solution.py:13
  539.9 24.2 %copy-start.42 = (bf16[128,1024]{1,0:T(8,128)(2,1)S(1)}, bf16[128,1024]{1,0:T(8,128)(2,1)}, u32[]{:S(2)}) copy-start(bf16[128,1024]{1,0:T(8,128)(2,1)} %copy-done.41) | copy-start | bytes 786436
  539.9 24.2 %copy-start.48 = (bf16[4,4,128,64]{2,3,1,0:T(8,128)(2,1)S(1)}, bf16[4,4,128,64]{2,3,1,0:T(8,128)(2,1)}, u32[]{:S(2)}) copy-start(bf16[4,4,128,64]{2,3,1,0:T(8,128)(2,1)} %get-tuple-element.196) | copy-start | bytes 786436
  539.9 22.4 %collective-permute-start.7 = (bf16[256,2048]{0,1:T(8,128)(2,1)S(1)}, bf16[256,2048]{0,1:T(8,128)(2,1)S(1)}, u32[]{:S(2)}, u32[]{:S(2)}) collective-permute-start(bf16[256,2048]{0,1:T(8,128)(2,1)S(1)} %select_convert_fusion.3), channel_id=1, source_target_pairs={{0,2},{1,3},{2,0},{3,1},{4,6},{5,7},{6,4},{7,5},{8,10},{9,11},{10,... | collective-permute-start | bytes 3145736 | tf_op jit(solution)/shard_map/ppermute | solution.py:13
  562.3 10.9 slice-start.2
  562.7 10.5 slice-start.3
  562.8 10.2 collective-permute-start.8
  564.1 12.0 slice-start.8
  594.6 415.1 %reduce-scatter.17.cloned.1.call-start = ((), (), s32[]{:S(2)}) async-start(), calls=%async_computation.8 | async-start | bytes 14155776 | tf_op jit(solution)/shard_map/reduce_scatter | solution.py:251
  635.9 117.7 %copy-start.4 = (f32[4,4,1024,64]{2,3,1,0:T(8,128)S(1)}, f32[4,4,1024,64]{2,3,1,0:T(8,128)}, u32[]{:S(2)}) copy-start(f32[4,4,1024,64]{2,3,1,0:T(8,128)} %get-tuple-element.203) | copy-start | bytes 12582916
  635.9 117.7 %copy-start.5 = (f32[4,4,1024,64]{2,3,1,0:T(8,128)S(1)}, f32[4,4,1024,64]{2,3,1,0:T(8,128)}, u32[]{:S(2)}) copy-start(f32[4,4,1024,64]{2,3,1,0:T(8,128)} %get-tuple-element.204) | copy-start | bytes 12582916
  640.1 113.5 %collective-permute-start.9 = (bf16[512,2048]{0,1:T(8,128)(2,1)S(1)}, bf16[512,2048]{0,1:T(8,128)(2,1)S(1)}, u32[]{:S(2)}, u32[]{:S(2)}) collective-permute-start(bf16[512,2048]{0,1:T(8,128)(2,1)S(1)} %select_convert_fusion), channel_id=1, source_target_pairs={{0,4},{1,5},{2,6},{3,7},{4,0},{5,1},{6,2},{7,3},{8,12},{9,13},{10,... | collective-permute-start | bytes 6291464 | tf_op jit(solution)/shard_map/ppermute | solution.py:13
  755.6 25.3 %copy-start.17 = (bf16[128,2048]{0,1:T(8,128)(2,1)S(1)}, bf16[128,2048]{0,1:T(8,128)(2,1)}, u32[]{:S(2)}) copy-start(bf16[128,2048]{0,1:T(8,128)(2,1)} %copy-done.16) | copy-start | bytes 1572868
  755.6 25.3 %copy-start.35 = (bf16[4,4,128,64]{2,3,1,0:T(8,128)(2,1)S(1)}, bf16[4,4,128,64]{2,3,1,0:T(8,128)(2,1)}, u32[]{:S(2)}) copy-start(bf16[4,4,128,64]{2,3,1,0:T(8,128)(2,1)} %get-tuple-element.198) | copy-start | bytes 786436
  755.6 23.6 %collective-permute-start.10 = (bf16[256,2048]{0,1:T(8,128)(2,1)S(1)}, bf16[256,2048]{0,1:T(8,128)(2,1)S(1)}, u32[]{:S(2)}, u32[]{:S(2)}) collective-permute-start(bf16[256,2048]{0,1:T(8,128)(2,1)S(1)} %select_convert_fusion.2), channel_id=1, source_target_pairs={{0,2},{1,3},{2,0},{3,1},{4,6},{5,7},{6,4},{7,5},{8,10},{9,11},{10,... | collective-permute-start | bytes 3145736 | tf_op jit(solution)/shard_map/ppermute | solution.py:13
  779.7 11.4 collective-permute-start.11
  798.4 497.5 %reduce-scatter.21.cloned.1.call-start = ((), (), s32[]{:S(2)}) async-start(), calls=%async_computation.10 | async-start | bytes 18874368 | tf_op jit(solution)/shard_map/reduce_scatter | solution.py:255
  811.4 769.8 %reduce-scatter.23.cloned.1.call-start = ((), (), s32[]{:S(2)}) async-start(), calls=%async_computation.11 | async-start | bytes 18874368 | tf_op jit(solution)/shard_map/reduce_scatter | solution.py:257
  823.2 820.6 %reduce-scatter.27.cloned.1.call-start = ((), (), s32[]{:S(2)}) async-start(), calls=%async_computation.13 | async-start | bytes 589824
  825.5 882.5 %reduce-scatter.29.cloned.1.call-start = ((), (), s32[]{:S(2)}) async-start(), calls=%async_computation.14 | async-start | bytes 589824
  826.7 946.0 %reduce-scatter.31.cloned.1.call-start = ((), (), s32[]{:S(2)}) async-start(), calls=%async_computation.15 | async-start | bytes 589824
  827.9 1009.1 %reduce-scatter.25.cloned.1.call-start = ((), (), s32[]{:S(2)}) async-start(), calls=%async_computation.12 | async-start | bytes 589824
  829.3 1081.4 %all-reduce.5.cloned.1.call-start = ((), (), s32[]{:S(2)}) async-start(), calls=%async_computation.16 | async-start | bytes 6291456 | tf_op jit(solution)/shard_map/psum | solution.py:314
  1583.9 189.7 %copy-start.22 = (f32[128,1024]{1,0:T(8,128)S(1)}, f32[128,1024]{1,0:T(8,128)}, u32[]{:S(2)}) copy-start(f32[128,1024]{1,0:T(8,128)} %copy-done.21) | copy-start | bytes 1572868
  (81 other events, 236.5 us)
Sparse Core Ops, SparseCore 0:
  594.7 124.8 reduce-scatter.18
  798.5 211.1 reduce-scatter.16
  1013.9 281.8 reduce-scatter.20
  1299.5 281.6 reduce-scatter.22
  1584.7 59.0 reduce-scatter.26
  1647.0 60.9 reduce-scatter.28
  1711.7 60.9 reduce-scatter.30
  1776.0 60.9 reduce-scatter.24
  1840.9 69.7 all-reduce.4
where the time goes:
time: 1930 us; the launch traced here: 1920 us
  waiting for transfers between devices  1530 us (79%)
  matrix products  181 us (9%)
  other arithmetic  73.9 us (4%)
  local copies, waits for them, and re-layouts  68.6 us (4%)
  blocking collectives  36.2 us (2%)
  starting transfers between devices  21.2 us (1%)
    ppermute x12, waiting for transfers between devices, from_partner(): lax.ppermute(x, axis, [(i, i ^ 1 << distance) for i in range(lax.axis_siz...  504 us
    reduce_scatter x1, waiting for transfers between devices, scatter_once(): lax.psum_scatter(in_grad, 'blk', scatter_dimension=0, tiled=True)  284 us
    reduce_scatter x1, waiting for transfers between devices, scatter_once(): lax.psum_scatter(back_grad, 'blk', scatter_dimension=1, tiled=True)  283 us
    unnamed x13, waiting for transfers between devices  214 us
    reduce_scatter x1, waiting for transfers between devices, scatter_once(): lax.psum_scatter(qkv_grad, 'blk', scatter_dimension=0, tiled=True)  179 us
    psum x1, waiting for transfers between devices, body(): lax.psum(qkv_part.astype(jnp.bfloat16), 'batch').astype(jnp.float32)  62.4 us
  transfers between devices with their start and end apart: 21, of which 20 were waited for; matrix products, arithmetic and copies ran while one was open for 6% of the time, Pallas kernels for 0%

commit v1 on v0

--- a/solution.py
+++ b/solution.py
@@ -1,6 +1,10 @@
+import functools
+
 import jax
 import jax.numpy as jnp
 from jax import lax
+from jax.experimental import pallas as pl
+from jax.experimental.pallas import tpu as pltpu
 from jax.sharding import PartitionSpec as P
 
 HEADS = 16
@@ -336,6 +340,370 @@
     )
 
 
+MESH = pl.DeviceIdType.MESH
+f32 = jnp.float32
+bf16 = jnp.bfloat16
+
+
+def member(j):
+    return {"blk": j}
+
+
+def place():
+    return lax.axis_index("blk")
+
+
+def exchange_kernel(group, columns, spread, src, dst, send_sem, recv_sem, own_sem):
+    me = place()
+    rows = 128
+    groups = columns // 128
+    barrier = pltpu.get_barrier_semaphore()
+    for step in range(1, group):
+        pl.semaphore_signal(
+            barrier, inc=1, device_id=member(lax.rem(me + step, group)), device_id_type=MESH
+        )
+    pl.semaphore_wait(barrier, group - 1)
+
+    def views(target, source):
+        for part in range(groups):
+            wide_t = pl.ds(pl.multiple_of(part * 128 * group + target * 128, 128), 128)
+            wide_s = pl.ds(pl.multiple_of(part * 128 * group + source * 128, 128), 128)
+            narrow = pl.ds(part * 128, 128)
+            row_s = pl.ds(pl.multiple_of(source * rows, rows), rows)
+            row_t = pl.ds(pl.multiple_of(target * rows, rows), rows)
+            if spread:
+                yield src.at[:, wide_t], dst.at[row_s, narrow]
+            else:
+                yield src.at[row_t, narrow], dst.at[:, wide_s]
+
+    copies = []
+    for step in range(1, group):
+        target = lax.rem(me + step, group)
+        for part, (here, there) in enumerate(views(target, me)):
+            copy = pltpu.make_async_remote_copy(
+                src_ref=here,
+                dst_ref=there,
+                send_sem=send_sem.at[step - 1, part],
+                recv_sem=recv_sem.at[step - 1, part],
+                device_id=member(target),
+                device_id_type=MESH,
+            )
+            copy.start()
+            copies.append(copy)
+    for part, (here, there) in enumerate(views(me, me)):
+        copy = pltpu.make_async_copy(here, there, own_sem.at[part])
+        copy.start()
+        copies.append(copy)
+    for copy in copies:
+        copy.wait()
+
+
+def exchange(x, group, spread, ident):
+    if spread:
+        groups = x.shape[1] // (128 * group)
+        out = (128 * group, groups * 128)
+    else:
+        groups = x.shape[1] // 128
+        out = (128, groups * 128 * group)
+    return pl.pallas_call(
+        functools.partial(exchange_kernel, group, groups * 128, spread),
+        out_shape=jax.ShapeDtypeStruct(out, x.dtype),
+        in_specs=[pl.BlockSpec(memory_space=pl.ANY)],
+        out_specs=pl.BlockSpec(memory_space=pl.ANY),
+        scratch_shapes=[
+            pltpu.SemaphoreType.DMA((group - 1, groups)),
+            pltpu.SemaphoreType.DMA((group - 1, groups)),
+            pltpu.SemaphoreType.DMA((groups,)),
+        ],
+        compiler_params=pltpu.CompilerParams(collective_id=ident, has_side_effects=True),
+    )(x)
+
+
+def dot_t(a, b):
+    return lax.dot_general(a, b, (((1,), (1,)), ((), ())), preferred_element_type=f32)
+
+
+def dot_0(a, b):
+    return lax.dot_general(a, b, (((0,), (0,)), ((), ())), preferred_element_type=f32)
+
+
+def attend_kernel(len_ref, qkv_ref, o_ref, lse_ref):
+    count = qkv_ref.shape[0]
+    limit = len_ref[0]
+    keys = qkv_ref[:, 128:256]
+    values = qkv_ref[:, 256:384]
+    low_half = lax.broadcasted_iota(jnp.int32, (1, 128), 1) < 64
+    valid = lax.broadcasted_iota(jnp.int32, (1, count), 1) < limit
+    step = 256
+    for start in range(0, count, step):
+        rows = pl.ds(start, step)
+        queries = qkv_ref[rows, 0:128]
+        outs, lses = [], []
+        for half in range(2):
+            mine = low_half if half == 0 else jnp.logical_not(low_half)
+            part = jnp.where(mine, queries, jnp.zeros_like(queries)) * jnp.asarray(0.125, bf16)
+            scores = jnp.where(valid, dot_t(part, keys), -1e30)
+            top = jnp.max(scores, axis=1, keepdims=True)
+            expd = jnp.exp(scores - top)
+            total = jnp.sum(expd, axis=1, keepdims=True)
+            probs = (expd * (1.0 / total)).astype(bf16)
+            outs.append(jnp.dot(probs, values, preferred_element_type=f32))
+            lses.append(top + jnp.log(total))
+        o_ref[rows, :] = jnp.where(low_half, outs[0], outs[1]).astype(bf16)
+        lse_ref[rows, :] = jnp.where(low_half, lses[0], lses[1])
+
+
+def attend(length, qkv):
+    count = qkv.shape[0]
+    return pl.pallas_call(
+        attend_kernel,
+        out_shape=(
+            jax.ShapeDtypeStruct((count, 128), bf16),
+            jax.ShapeDtypeStruct((count, 128), f32),
+        ),
+        in_specs=[
+            pl.BlockSpec(memory_space=pltpu.SMEM),
+            pl.BlockSpec(memory_space=pltpu.VMEM),
+        ],
+        out_specs=(
+            pl.BlockSpec(memory_space=pltpu.VMEM),
+            pl.BlockSpec(memory_space=pltpu.VMEM),
+        ),
+        compiler_params=pltpu.CompilerParams(vmem_limit_bytes=48 * 2**20),
+        cost_estimate=pl.CostEstimate(
+            flops=4 * count * count * 128, bytes_accessed=count * 2048, transcendentals=2 * count * count
+        ),
+    )(length, qkv)
+
+
+def attend_back_kernel(len_ref, qkv_ref, do_ref, lse_ref, dqkv_ref, dk_ref, dv_ref):
+    count = qkv_ref.shape[0]
+    limit = len_ref[0]
+    keys = qkv_ref[:, 128:256]
+    values = qkv_ref[:, 256:384]
+    low_half = lax.broadcasted_iota(jnp.int32, (1, 128), 1) < 64
+    valid = lax.broadcasted_iota(jnp.int32, (1, count), 1) < limit
+    step = 256
+    for start in range(0, count, step):
+        rows = pl.ds(start, step)
+        queries = qkv_ref[rows, 0:128]
+        grads = do_ref[rows, :]
+        lse = lse_ref[rows, :]
+        dqs, dks, dvs = [], [], []
+        for half in range(2):
+            mine = low_half if half == 0 else jnp.logical_not(low_half)
+            q_part = jnp.where(mine, queries, jnp.zeros_like(queries)) * jnp.asarray(0.125, bf16)
+            g_part = jnp.where(mine, grads, jnp.zeros_like(grads))
+            scores = dot_t(q_part, keys)
+            probs = jnp.where(valid, jnp.exp(scores - lse[:, 64 * half : 64 * half + 1]), 0.0)
+            dp = dot_t(g_part, values)
+            delta = jnp.sum(probs * dp, axis=1, keepdims=True)
+            ds = (probs * (dp - delta)).astype(bf16)
+            dqs.append(jnp.dot(ds, keys, preferred_element_type=f32))
+            dks.append(dot_0(ds, q_part))
+            dvs.append(dot_0(probs.astype(bf16), g_part))
+        dqkv_ref[rows, 0:128] = (jnp.where(low_half, dqs[0], dqs[1]) * 0.125).astype(bf16)
+        dk = dks[0] + dks[1]
+        dv = dvs[0] + dvs[1]
+        if start == 0:
+            dk_ref[...] = dk
+            dv_ref[...] = dv
+        else:
+            dk_ref[...] += dk
+            dv_ref[...] += dv
+    dqkv_ref[:, 128:256] = dk_ref[...].astype(bf16)
+    dqkv_ref[:, 256:384] = dv_ref[...].astype(bf16)
+
+
+def attend_back(length, qkv, grads, lse):
+    count = qkv.shape[0]
+    return pl.pallas_call(
+        attend_back_kernel,
+        out_shape=jax.ShapeDtypeStruct((count, 384), bf16),
+        in_specs=[pl.BlockSpec(memory_space=pltpu.SMEM)]
+        + [pl.BlockSpec(memory_space=pltpu.VMEM)] * 3,
+        out_specs=pl.BlockSpec(memory_space=pltpu.VMEM),
+        scratch_shapes=[pltpu.VMEM((count, 128), f32), pltpu.VMEM((count, 128), f32)],
+        compiler_params=pltpu.CompilerParams(vmem_limit_bytes=48 * 2**20),
+        cost_estimate=pl.CostEstimate(
+            flops=10 * count * count * 128, bytes_accessed=count * 3072, transcendentals=2 * count * count
+        ),
+    )(length, qkv, grads, lse)
+
+
+def fast_forward(hidden, params, length, group):
+    w_qkv, qv_bias, w_attn, out_bias, w_in, in_bias, w_back, norm_gain, norm_shift = params
+    hidden_low = hidden.astype(bf16)
+    bias_row = jnp.concatenate([qv_bias[0], jnp.zeros_like(qv_bias[0]), qv_bias[1]])
+    projected = (jnp.dot(hidden_low, w_qkv, preferred_element_type=f32) + bias_row).astype(bf16)
+    qkv = exchange(projected, group, True, 1)
+    heads_out, lse = attend(length, qkv)
+    attended = exchange(heads_out, group, False, 2)
+    first_sum = hidden + jnp.dot(attended, w_attn, preferred_element_type=f32) + out_bias[0]
+    first_norm = normalize(first_sum, norm_gain[0], norm_shift[0])
+    first_low = first_norm.astype(bf16)
+    inner_pre = jnp.dot(first_low, w_in, preferred_element_type=f32) + in_bias
+    activated = gelu_exact(inner_pre).astype(bf16)
+    second_sum = first_norm + jnp.dot(activated, w_back, preferred_element_type=f32) + out_bias[1]
+    output = normalize(second_sum, norm_gain[1], norm_shift[1])
+    return output, (
+        hidden_low, qkv, lse, attended, first_sum, first_low, inner_pre, activated, second_sum,
+    )
+
+
+def back_normalize(values, gain, grad):
+    centered = values - jnp.mean(values, axis=-1, keepdims=True)
+    inverse = lax.rsqrt(jnp.mean(centered * centered, axis=-1, keepdims=True) + eps)
+    unit = centered * inverse
+    scaled = grad * gain
+    inner = jnp.mean(scaled * unit, axis=-1, keepdims=True)
+    return (
+        inverse * (scaled - jnp.mean(scaled, axis=-1, keepdims=True) - unit * inner),
+        jnp.sum(grad * unit, axis=0),
+        jnp.sum(grad, axis=0),
+    )
+
+
+def fast_backward(grad_output, saved, params, length, group):
+    w_qkv, qv_bias, w_attn, out_bias, w_in, in_bias, w_back, norm_gain, norm_shift = params
+    hidden_low, qkv, lse, attended, first_sum, first_low, inner_pre, activated, second_sum = saved
+    grad_second, gain_two, shift_two = back_normalize(second_sum, norm_gain[1], grad_output)
+    dz_two = grad_second.astype(bf16)
+    grad_act = dot_t(dz_two, w_back)
+    unused_gelu, pull_gelu = jax.vjp(gelu_exact, inner_pre)
+    du = pull_gelu(grad_act)[0].astype(bf16)
+    grad_first_norm = grad_second + dot_t(du, w_in)
+    grad_first, gain_one, shift_one = back_normalize(first_sum, norm_gain[0], grad_first_norm)
+    dz = grad_first.astype(bf16)
+    grad_attended = dot_t(dz, w_attn).astype(bf16)
+    head_grads = exchange(grad_attended, group, True, 3)
+    dqkv_heads = attend_back(length, qkv, head_grads, lse)
+    dqkv = exchange(dqkv_heads, group, False, 4)
+    grad_hidden = grad_first + dot_t(dqkv, w_qkv)
+
+    def column_sum(x):
+        return jnp.sum(x.astype(f32), axis=0)
+
+    width = hidden_low.shape[1]
+    sums = column_sum(dqkv)
+    vectors = (
+        sums[:width], sums[2 * width :], column_sum(dz), column_sum(dz_two), column_sum(du),
+        gain_one, gain_two, shift_one, shift_two,
+    )
+    pairs = ((hidden_low, dqkv), (attended, dz), (first_low, du), (dz_two, activated))
+    return grad_hidden, vectors, pairs
+
+
+def swap(x, axis, bit):
+    return from_partner(x, axis, bit)
+
+
+def add_low(kept, received):
+    return (kept.astype(f32) + received.astype(f32)).astype(bf16)
+
+
+def pick(x, at, axis):
+    return lax.dynamic_index_in_dim(x, at, axis, keepdims=False)
+
+
+def fold(x, axis, index, mesh_axis, bit):
+    sent = pick(x, 1 - index, axis)
+    kept = pick(x, index, axis)
+    return add_low(kept, swap(sent, mesh_axis, bit))
+
+
+def join(x, index, mesh_axis, bit):
+    other = swap(x, mesh_axis, bit)
+    return jnp.where(index == 0, jnp.stack([x, other]), jnp.stack([other, x]))
+
+
+def reduce_yxz(total, position, row):
+    columns = total.shape[1]
+    z_hi, z_lo, y = position >> 2, position >> 1 & 1, position & 1
+    x_at = row >> 1
+    cut = total.reshape(2, 2, 2, 128, columns)
+    part = fold(cut, 2, y, "blk", 0)
+    part = part.reshape(2, 2, 2, 64, columns)
+    part = fold(part, 2, x_at, "batch", 1)
+    part = fold(part, 1, z_lo, "blk", 1)
+    part = fold(part, 0, z_hi, "blk", 2)
+    return join(part, x_at, "batch", 1).reshape(128, columns)
+
+
+def reduce_zyx(total, position, row):
+    columns = total.shape[1]
+    z_hi, z_lo, y = position >> 2, position >> 1 & 1, position & 1
+    cut = total.reshape(2, 2, 2, 128, columns)
+    part = fold(cut, 1, z_lo, "blk", 1)
+    part = fold(part, 0, z_hi, "blk", 2)
+    part = fold(part, 0, y, "blk", 0)
+    return add_low(part, swap(part, "batch", 1))
+
+
+def fast_body(tokens, lengths, *rest):
+    params, cotangent = rest[:-1], rest[-1]
+    group = lax.axis_size("blk")
+    position = lax.axis_index("blk")
+    row = lax.axis_index("batch")
+    core = row & 1
+    out_one, saved_one = fast_forward(tokens[0].astype(f32), params, lengths, group)
+    out_two, saved_two = fast_forward(out_one, params, lengths, group)
+    grad, vec_two, pairs_two = fast_backward(cotangent[0].astype(f32), saved_two, params, lengths, group)
+    grad, vec_one, pairs_one = fast_backward(grad, saved_one, params, lengths, group)
+
+    def half_grad(pair_two, pair_one):
+        def both(two, one, split):
+            mine = jnp.concatenate([two, one], 0)
+            if split:
+                halves = mine.reshape(mine.shape[0], 2, mine.shape[1] // 2)
+                mine, sent = pick(halves, core, 1), pick(halves, 1 - core, 1)
+            else:
+                sent = mine
+            return jnp.concatenate([mine, swap(sent, "batch", 0)], 0)
+
+        left = both(pair_two[0], pair_one[0], False)
+        right = both(pair_two[1], pair_one[1], True)
+        return dot_0(left, right).astype(bf16)
+
+    qkv_half, attn_half, in_half, back_half = [
+        half_grad(two, one) for two, one in zip(pairs_two, pairs_one)
+    ]
+    vectors = [a + b for a, b in zip(vec_two, vec_one)]
+    stacked = jnp.concatenate(
+        [jnp.stack(vectors[:4] + vectors[5:]).reshape(8, 8, 128),
+         vectors[4].reshape(8, 4, 128).transpose(1, 0, 2)], 0
+    )
+    pieces = stacked.transpose(1, 2, 0).reshape(1024, 12)
+    pieces = pieces + swap(pieces, "batch", 0)
+    pieces = jnp.pad(pieces, ((0, 0), (0, 116))).astype(bf16)
+    back_part = reduce_yxz(back_half, position, row)
+    in_part = reduce_yxz(in_half, position, row)
+    tail = reduce_zyx(jnp.concatenate([attn_half, qkv_half, pieces], 1), position, row)
+
+    def whole(part):
+        both = join(part, core, "batch", 0)
+        return both.transpose(1, 0, 2).reshape(128, -1).astype(f32)
+
+    back_grad = whole(back_part).T
+    in_grad = whole(in_part)
+    attn_grad = whole(tail[:, :512])
+    qkv_grad = whole(tail[:, 512:2048])
+    small = tail[:, 2048:2060].astype(f32).T
+    return (
+        out_two.astype(bf16)[None],
+        grad.astype(bf16)[None],
+        qkv_grad,
+        small[0:2],
+        attn_grad,
+        small[2:4],
+        in_grad,
+        small[8:12].reshape(512),
+        back_grad,
+        small[4:6],
+        small[6:8],
+    )
+
+
 def solution(mesh):
     placed = (
         P("batch", "blk", None),
@@ -351,8 +719,9 @@
         P(),
         P("batch", "blk", None),
     )
+    fast = dict(mesh.shape) == {"batch": 4, "blk": 8}
     return jax.shard_map(
-        body,
+        fast_body if fast else body,
         mesh=mesh,
         in_specs=placed,
         out_specs=(

time: 1930 us -> 485 us (0.25)
  waiting for transfers between devices: 1530 us -> 119 us
  Pallas kernels: 0 us -> 131 us
  matrix products: 181 us -> 78.4 us
  other arithmetic: 73.9 us -> 30.4 us
  blocking collectives: 36.2 us -> 0 us
    reduce_scatter x4 -> x0, waiting for transfers between devices: 745 us -> none  [the longest x1 284 us: scatter_once(): lax.psum_scatter(in_grad, 'blk', scatter_dimension=0, tiled=True)]
    ppermute x12 -> x27, waiting for transfers between devices: 504 us -> 119 us  [from_partner(): lax.ppermute(x, axis, [(i, i ^ 1 << distance) for i in range(lax.axis_siz...]
    unnamed x13 -> x0, waiting for transfers between devices: 214 us -> none
    pallas_call x0 -> x12, Pallas kernels: none -> 131 us  [the longest x8 105 us: exchange(): pl.pallas_call(functools.partial(exchange_kernel, group, groups * 128, sp...]
    dot_general x80 -> x20, matrix products: 181 us -> 78.4 us  [the longest x8 30.8 us: dot_t(): lax.dot_general(a, b, (((1,), (1,)), ((), ())), preferred_element_type=f32)]
    psum x1 -> x0, waiting for transfers between devices: 62.4 us -> none  [body(): lax.psum(qkv_part.astype(jnp.bfloat16), 'batch').astype(jnp.float32)]
    unnamed x1 -> x0, blocking collectives: 28.6 us -> none
    dynamic_slice x0 -> x8, local copies, waits for them, and re-layouts: none -> 25.4 us  [pick(): return lax.dynamic_index_in_dim(x, at, axis, keepdims=False)]
  transfers between devices with their start and end apart: 21 -> 27, of which waited for: 20 -> 7; matrix products, arithmetic and copies ran while one was open for 6% -> 22% of each run, Pallas kernels for 0% -> 0%
where the time goes in v1:
time: 485 us; the launch traced here: 479 us
  Pallas kernels  131 us (27%)
  waiting for transfers between devices  119 us (25%)
  local copies, waits for them, and re-layouts  85.6 us (18%)
  matrix products  78.4 us (16%)
  starting transfers between devices  30.5 us (6%)
  other arithmetic  30.4 us (6%)
    ppermute x27, waiting for transfers between devices, from_partner(): lax.ppermute(x, axis, [(i, i ^ 1 << distance) for i in range(lax.axis_siz...  119 us
    pallas_call x8, Pallas kernels, exchange(): pl.pallas_call(functools.partial(exchange_kernel, group, groups * 128, sp...  105 us
    unnamed x170, local copies, waits for them, and re-layouts  34.5 us
    dot_general x8, matrix products, dot_t(): lax.dot_general(a, b, (((1,), (1,)), ((), ())), preferred_element_type=f32)  30.8 us
    ppermute x27, starting transfers between devices, from_partner(): lax.ppermute(x, axis, [(i, i ^ 1 << distance) for i in range(lax.axis_siz...  30.5 us
    dynamic_slice x8, local copies, waits for them, and re-layouts, pick(): return lax.dynamic_index_in_dim(x, at, axis, keepdims=False)  25.4 us
    dot_general x2, matrix products, fast_forward(): inner_pre = jnp.dot(first_low, w_in, preferred_element_type=f32) + in_bias  20.2 us
    pallas_call x2, Pallas kernels, attend_back(): pl.pallas_call(attend_back_kernel, out_shape=jax.ShapeDtypeStruct((count,...  16.3 us
  transfers between devices with their start and end apart: 27, of which 7 were waited for; matrix products, arithmetic and copies ran while one was open for 22% of the time, Pallas kernels for 0%

profile of v1, /device:TPU:1, one launch (start us, length us, event | category | flops | bytes accessed | tf_op | source)
XLA Modules:
  0.0 478.5 jit_solution(7718490950930262139)
XLA Ops:
  3.0 4.8 fusion.5.src
  7.8 17.9 %shard_map.203.qkv_ref = bf16[1024,384]{1,0:T(8,128)(2,1)} custom-call(bf16[128,3072]{1,0:T(8,128)(2,1)} %fusion.5.src), custom_call_target="tpu_custom_call" | custom-call | tf_op jit(solution)/shard_map/pallas_call | solution.py:408
  26.8 5.2 %shard_map.204 = (bf16[1024,128]{1,0:T(8,128)(2,1)S(1)}, f32[1024,128]{1,0:T(8,128)S(1)}) custom-call(s32[1]{0:T(128)S(6)} %copy.117.len_ref, bf16[1024,384]{1,0:T(8,128)(2,1)S(1)} %copy-done.2), custom_call_target="tpu_custom_call" | custom-call | flops 536870912 | bytes 2097152 | tf_op jit(solution)/shard_map/pallas_call | solution.py:458
  32.7 11.4 %shard_map.205 = bf16[128,1024]{1,0:T(8,128)(2,1)} custom-call(bf16[1024,128]{1,0:T(8,128)(2,1)} %copy-done.10), custom_call_target="tpu_custom_call" | custom-call | tf_op jit(solution)/shard_map/pallas_call | solution.py:408
  46.1 10.5 %multiply_convert_fusion.1 = (bf16[128,4096]{1,0:T(8,128)(2,1)S(1)}, f32[128,4096]{1,0:T(8,128)}, f32[128,4096]{1,0:T(8,128)}) fusion(f32[4096]{0:T(1024)S(1)} %copy-done.64, bf16[128,1024]{1,0:T(8,128)(2,1)S(1)} %fusion.75, bf16[1024,4096]{1,0:T(8,128)(2,1)} %param.18), kind=kOutput, calls=%fused_computation.57 | convolution fusion | flops 1108344832 | bytes 13910016 | tf_op jit(solution)/shard_map/dot_general | solution.py:545
  61.9 14.9 %shard_map.206.qkv_ref = bf16[1024,384]{1,0:T(8,128)(2,1)} custom-call(bf16[128,3072]{1,0:T(8,128)(2,1)} %fusion.6.src), custom_call_target="tpu_custom_call" | custom-call | tf_op jit(solution)/shard_map/pallas_call | solution.py:408
  78.0 5.2 %shard_map.207 = (bf16[1024,128]{1,0:T(8,128)(2,1)S(1)}, f32[1024,128]{1,0:T(8,128)S(1)}) custom-call(s32[1]{0:T(128)S(6)} %copy.117.len_ref, bf16[1024,384]{1,0:T(8,128)(2,1)S(1)} %copy-done.4), custom_call_target="tpu_custom_call" | custom-call | flops 536870912 | bytes 2097152 | tf_op jit(solution)/shard_map/pallas_call | solution.py:458
  83.9 13.4 %shard_map.208 = bf16[128,1024]{1,0:T(8,128)(2,1)} custom-call(bf16[1024,128]{1,0:T(8,128)(2,1)} %copy-done.11), custom_call_target="tpu_custom_call" | custom-call | tf_op jit(solution)/shard_map/pallas_call | solution.py:408
  99.7 9.7 %multiply_convert_fusion = (bf16[128,4096]{1,0:T(8,128)(2,1)S(1)}, f32[128,4096]{1,0:T(8,128)}, f32[128,4096]{1,0:T(8,128)}) fusion(f32[4096]{0:T(1024)S(1)} %copy-done.64, bf16[128,1024]{1,0:T(8,128)(2,1)S(1)} %fusion.77, bf16[1024,4096]{1,0:T(8,128)(2,1)} %param.18), kind=kOutput, calls=%fused_computation.44 | convolution fusion | flops 1108344832 | bytes 13910016 | tf_op jit(solution)/shard_map/dot_general | solution.py:545
  112.6 5.8 %convert_reduce_fusion.1 = (f32[4096]{0:T(1024)S(1)}, bf16[128,4096]{1,0:T(8,128)(2,1)S(1)}) fusion(f32[128,4096]{1,0:T(8,128)} %get-tuple-element.72, f32[128,4096]{1,0:T(8,128)} %get-tuple-element.113, bf16[128,1024]{1,0:T(8,128)(2,1)S(1)} %get-tuple-element.64, bf16[4096,1024]{1,0:T(8,128)(2,1)S(1)} %bitcast.233), kind=kOutput, calls=%fused_computation.41 | convolution fusion | flops 1082126336 | bytes 13910016 | tf_op jit(solution)/shard_map/dot_general | solution.py:423
  118.4 3.1 multiply_reduce_fusion.2
  124.8 7.3 %shard_map.209.do_ref = bf16[1024,128]{1,0:T(8,128)(2,1)} custom-call(bf16[128,1024]{1,0:T(8,128)(2,1)} %convolution_convert_fusion.5.src), custom_call_target="tpu_custom_call" | custom-call | tf_op jit(solution)/shard_map/pallas_call | solution.py:408
  134.1 8.0 %shard_map.210.src = bf16[1024,384]{1,0:T(8,128)(2,1)S(1)} custom-call(s32[1]{0:T(128)S(6)} %copy.117.len_ref, bf16[1024,384]{1,0:T(8,128)(2,1)S(1)} %copy-done.5, bf16[1024,128]{1,0:T(8,128)(2,1)S(1)} %copy-done.9, f32[1024,128]{1,0:T(8,128)S(1)} %copy-done.13), custom_call_target="tpu_custom_call" | custom-call | flops 1342177280 | bytes 3145728 | tf_op jit(solution)/shard_map/pallas_call | solution.py:520
  143.0 12.8 %shard_map.211 = bf16[128,3072]{1,0:T(8,128)(2,1)} custom-call(bf16[1024,384]{1,0:T(8,128)(2,1)} %copy-done.7), custom_call_target="tpu_custom_call" | custom-call | tf_op jit(solution)/shard_map/pallas_call | solution.py:408
  157.2 5.6 %multiply_reduce_fusion = (f32[1024]{0:T(1024)S(1)}, f32[128]{0:T(128)S(1)}, f32[128]{0:T(128)S(1)}, f32[1024]{0:T(1024)S(1)}, f32[128,1024]{1,0:T(8,128)S(1)}) fusion(f32[128,1024]{1,0:T(8,128)S(1)} %copy-done.17, f32[128]{0:T(128)S(1)} %add_rsqrt_fusion.2, f32[128]{0:T(128)S(1)} %broadcast_multiply_fusion.10, f32[1024]{0:T(1024)S(1)} %bitcast.278, ...), kind=kOutput, calls=%fused_computation.165 | convolution fusion | flops 806614784 | bytes 8665088 | tf_op jit(solution)/shard_map/dot_general | solution.py:423
  163.1 7.0 %convert_reduce_fusion = (f32[4096]{0:T(1024)S(1)}, bf16[128,4096]{1,0:T(8,128)(2,1)S(1)}) fusion(f32[128,4096]{1,0:T(8,128)S(1)} %copy-done.65, f32[128,4096]{1,0:T(8,128)S(1)} %copy-done.66, bf16[128,1024]{1,0:T(8,128)(2,1)S(1)} %get-tuple-element.61, bf16[4096,1024]{1,0:T(8,128)(2,1)} %param.20), kind=kOutput, calls=%fused_computation.40 | convolution fusion | flops 1082126336 | bytes 13910016 | tf_op jit(solution)/shard_map/dot_general | solution.py:423
  170.2 3.1 multiply_reduce_fusion.1
  176.5 14.3 %shard_map.212.do_ref = bf16[1024,128]{1,0:T(8,128)(2,1)} custom-call(bf16[128,1024]{1,0:T(8,128)(2,1)} %convolution_convert_fusion.4.src), custom_call_target="tpu_custom_call" | custom-call | tf_op jit(solution)/shard_map/pallas_call | solution.py:408
  191.8 8.3 %shard_map.213.src = bf16[1024,384]{1,0:T(8,128)(2,1)S(1)} custom-call(s32[1]{0:T(128)S(6)} %copy.117.len_ref, bf16[1024,384]{1,0:T(8,128)(2,1)S(1)} %copy-done.3, bf16[1024,128]{1,0:T(8,128)(2,1)S(1)} %copy-done.8, f32[1024,128]{1,0:T(8,128)S(1)} %get-tuple-element.18.lse_ref), custom_call_target="tpu_custom_call" | custom-call | flops 1342177280 | bytes 3145728 | tf_op jit(solution)/shard_map/pallas_call | solution.py:520
  201.0 12.5 %shard_map.214 = bf16[128,3072]{1,0:T(8,128)(2,1)} custom-call(bf16[1024,384]{1,0:T(8,128)(2,1)} %copy-done.6), custom_call_target="tpu_custom_call" | custom-call | tf_op jit(solution)/shard_map/pallas_call | solution.py:408
  216.0 5.6 %collective-permute-start.4 = (f32[1024,12]{1,0:T(8,128)}, f32[1024,12]{1,0:T(8,128)}, u32[]{:S(2)}, u32[]{:S(2)}) collective-permute-start(f32[1024,12]{1,0:T(8,128)} %bitcast.35), channel_id=1, source_target_pairs={{0,8},{8,0},{16,24},{24,16},{1,9},{9,1},{17,25},{25,17},{2,10},{10... | collective-permute-start | bytes 147464 | tf_op jit(solution)/shard_map/ppermute | solution.py:17
  222.9 4.2 reshape.390
  227.1 4.4 constant_dynamic-slice_fusion.9
  241.4 3.3 reshape.393
  244.7 6.3 %constant_dynamic-slice_fusion.5 = (bf16[256,1,2048]{2,1,0:T(2,128)(2,1)}, bf16[256,1,2048]{2,1,0:T(2,128)(2,1)}) fusion(bf16[256,2,2048]{2,1,0:T(2,128)(2,1)S(1)} %reshape.393, s32[]{:T(128)S(6)} %select_n.129, s32[]{:T(128)S(6)} %select_n.130), kind=kLoop, calls=%fused_computation.210 | loop fusion | bytes 4194312 | tf_op jit(solution)/shard_map/jit(dynamic_index_in_dim)/dynamic_slice | solution.py:606
  252.0 2.5 copy.114
  256.8 3.3 reshape.397
  262.9 3.1 convolution_convert_fusion.3
  268.2 3.5 convolution_convert_fusion.2
  274.5 4.5 copy.70
  279.1 4.5 collective-permute-start.5
  283.6 5.6 %constant_dynamic-slice_fusion.3 = (bf16[256,1,2048]{2,1,0:T(2,128)(2,1)}, bf16[256,1,2048]{2,1,0:T(2,128)(2,1)S(1)}) fusion(bf16[256,2,2048]{2,1,0:T(2,128)(2,1)S(1)} %reshape.397, s32[]{:T(128)S(6)} %select_n.129, s32[]{:T(128)S(6)} %select_n.130), kind=kLoop, calls=%fused_computation.208 | loop fusion | bytes 4194312 | tf_op jit(solution)/shard_map/jit(dynamic_index_in_dim)/dynamic_slice | solution.py:606
  295.7 3.9 convolution_convert_fusion.1
  304.5 3.9 convolution_convert_fusion
  311.1 3.2 fusion.36
  314.3 4.1 copy.88
  318.4 13.9 %collective-permute-done.5 = bf16[2,2,128,2176]{2,3,1,0:T(8,128)(2,1)} collective-permute-done((bf16[2,2,128,2176]{2,3,1,0:T(8,128)(2,1)}, bf16[2,2,128,2176]{2,3,1,0:T(8,128)(2,1)}, u32[]{:S(2)}, u32[]{:S(2)}) %collective-permute-start.5) | collective-permute-done | bytes 2228256 | tf_op jit(solution)/shard_map/ppermute | solution.py:17
  332.3 3.0 fusion.2
  337.6 12.6 %collective-permute-done.13 = bf16[2,2,128,2048]{3,2,1,0:T(8,128)(2,1)S(1)} collective-permute-done((bf16[2,2,128,2048]{3,2,1,0:T(8,128)(2,1)}, bf16[2,2,128,2048]{3,2,1,0:T(8,128)(2,1)S(1)}, u32[]{:S(2)}, u32[]{:S(2)}) %collective-permute-start.13) | collective-permute-done | bytes 2097184 | tf_op jit(solution)/shard_map/ppermute | solution.py:17
  352.5 42.7 %collective-permute-done.21 = bf16[2,2,128,2048]{3,2,1,0:T(8,128)(2,1)} collective-permute-done((bf16[2,2,128,2048]{3,2,1,0:T(8,128)(2,1)}, bf16[2,2,128,2048]{3,2,1,0:T(8,128)(2,1)}, u32[]{:S(2)}, u32[]{:S(2)}) %collective-permute-start.21) | collective-permute-done | bytes 2097184 | tf_op jit(solution)/shard_map/ppermute | solution.py:17
  395.3 2.5 fusion.3
  401.4 20.3 %collective-permute-done.22 = bf16[2,2,64,2048]{3,2,0,1:T(8,128)(2,1)S(1)} collective-permute-done((bf16[2,2,64,2048]{3,2,0,1:T(8,128)(2,1)S(1)}, bf16[2,2,64,2048]{3,2,0,1:T(8,128)(2,1)S(1)}, u32[]{:S(2)}, u32[]{:S(2)}) %collective-permute-start.22) | collective-permute-done | bytes 1048608 | tf_op jit(solution)/shard_map/ppermute | solution.py:17
  425.9 13.3 %collective-permute-done.23 = bf16[2,64,2048]{2,1,0:T(8,128)(2,1)S(1)} collective-permute-done((bf16[2,64,2048]{2,1,0:T(8,128)(2,1)S(1)}, bf16[2,64,2048]{2,1,0:T(8,128)(2,1)S(1)}, u32[]{:S(2)}, u32[]{:S(2)}) %collective-permute-start.23) | collective-permute-done | bytes 524320 | tf_op jit(solution)/shard_map/ppermute | solution.py:17
  441.5 13.1 %collective-permute-done.24 = bf16[64,2048]{1,0:T(8,128)(2,1)S(1)} collective-permute-done((bf16[64,2048]{1,0:T(8,128)(2,1)S(1)}, bf16[64,2048]{1,0:T(8,128)(2,1)S(1)}, u32[]{:S(2)}, u32[]{:S(2)}) %collective-permute-start.24) | collective-permute-done | bytes 262176 | tf_op jit(solution)/shard_map/ppermute | solution.py:17
  458.8 3.3 collective-permute-done.25
  469.7 2.9 copy.83
  472.6 2.9 convert_bitcast_fusion
  475.4 2.9 copy.80
  (317 shorter events, 95.4 us)
Async XLA Ops:
  0.6 43.5 %copy-start = (bf16[1024,1024]{1,0:T(8,128)(2,1)S(1)}, bf16[1024,1024]{1,0:T(8,128)(2,1)}, u32[]{:S(2)}) copy-start(bf16[1024,1024]{1,0:T(8,128)(2,1)} %param.16) | copy-start | bytes 6291460
  26.8 17.3 %copy-start.62 = (f32[2,1024]{1,0:T(2,128)S(1)}, f32[2,1024]{1,0:T(2,128)}, u32[]{:S(2)}) copy-start(f32[2,1024]{1,0:T(2,128)} %param.22) | copy-start | bytes 24580
  26.8 17.4 %copy-start.63 = (f32[2,1024]{1,0:T(2,128)S(1)}, f32[2,1024]{1,0:T(2,128)}, u32[]{:S(2)}) copy-start(f32[2,1024]{1,0:T(2,128)} %param.21) | copy-start | bytes 24580
  26.8 17.4 %copy-start.39 = (bf16[1,128,1024]{2,1,0:T(8,128)(2,1)S(1)}, bf16[1,128,1024]{2,1,0:T(8,128)(2,1)}, u32[]{:S(2)}) copy-start(bf16[1,128,1024]{2,1,0:T(8,128)(2,1)} %param.12) | copy-start | bytes 786436
  45.7 10.9 %copy-start.14 = (f32[128,1024]{1,0:T(8,128)}, f32[128,1024]{1,0:T(8,128)S(1)}, u32[]{:S(2)}) copy-start(f32[128,1024]{1,0:T(8,128)S(1)} %get-tuple-element.107) | copy-start | bytes 1572868
  45.7 10.9 %slice-start.4 = ((s8[8388608]{0:T(1024)(128)(4,1)}), s8[4194304]{0:T(1024)(128)(4,1)S(1)}, s32[]{:S(2)}) async-start(s8[8388608]{0:T(1024)(128)(4,1)} %bitcast.230), calls=%async_computation.4 | async-start | bytes 8388608
  46.1 10.5 %copy-start.52 = (bf16[128,1024]{1,0:T(8,128)(2,1)}, bf16[128,1024]{1,0:T(8,128)(2,1)S(1)}, u32[]{:S(2)}) copy-start(bf16[128,1024]{1,0:T(8,128)(2,1)S(1)} %fusion.75) | copy-start | bytes 786436
  46.1 10.5 %slice-start.5 = ((s8[8388608]{0:T(1024)(128)(4,1)}), s8[4194304]{0:T(1024)(128)(4,1)S(1)}, s32[]{:S(2)}) async-start(s8[8388608]{0:T(1024)(128)(4,1)} %bitcast.230), calls=%async_computation.5 | async-start | bytes 8388608
  83.9 15.6 %copy-start.12 = (f32[1024,128]{1,0:T(8,128)}, f32[1024,128]{1,0:T(8,128)S(1)}, u32[]{:S(2)}) copy-start(f32[1024,128]{1,0:T(8,128)S(1)} %get-tuple-element.17.lse_ref) | copy-start | bytes 1572868
  97.4 12.1 %slice-start.6 = ((s8[8388608]{0:T(1024)(128)(4,1)}), s8[4194304]{0:T(1024)(128)(4,1)S(1)}, s32[]{:S(2)}) async-start(s8[8388608]{0:T(1024)(128)(4,1)} %bitcast.232), calls=%async_computation.6 | async-start | bytes 8388608
  99.7 9.8 %copy-start.55 = (bf16[128,1024]{1,0:T(8,128)(2,1)}, bf16[128,1024]{1,0:T(8,128)(2,1)S(1)}, u32[]{:S(2)}) copy-start(bf16[128,1024]{1,0:T(8,128)(2,1)S(1)} %fusion.77) | copy-start | bytes 786436
  99.7 9.8 %slice-start.7 = ((s8[8388608]{0:T(1024)(128)(4,1)}), s8[4194304]{0:T(1024)(128)(4,1)S(1)}, s32[]{:S(2)}) async-start(s8[8388608]{0:T(1024)(128)(4,1)} %bitcast.232), calls=%async_computation.7 | async-start | bytes 8388608
  121.6 10.5 %copy-start.5 = (bf16[1024,384]{1,0:T(8,128)(2,1)S(1)}, bf16[1024,384]{1,0:T(8,128)(2,1)}, u32[]{:S(2)}) copy-start(bf16[1024,384]{1,0:T(8,128)(2,1)} %shard_map.206.qkv_ref) | copy-start | bytes 2359300
  143.0 14.1 %copy-start.17 = (f32[128,1024]{1,0:T(8,128)S(1)}, f32[128,1024]{1,0:T(8,128)}, u32[]{:S(2)}) copy-start(f32[128,1024]{1,0:T(8,128)} %copy-done.16) | copy-start | bytes 1572868
  157.2 13.0 %slice-start.10 = ((s8[8388608]{0:T(1024)(128)(4,1)}), s8[4194304]{0:T(1024)(128)(4,1)S(1)}, s32[]{:S(2)}) async-start(s8[8388608]{0:T(1024)(128)(4,1)} %bitcast.236), calls=%async_computation.10 | async-start | bytes 8388608
  173.3 17.6 %copy-start.3 = (bf16[1024,384]{1,0:T(8,128)(2,1)S(1)}, bf16[1024,384]{1,0:T(8,128)(2,1)}, u32[]{:S(2)}) copy-start(bf16[1024,384]{1,0:T(8,128)(2,1)} %shard_map.203.qkv_ref) | copy-start | bytes 2359300
  201.0 20.7 %copy-start.18 = (bf16[128,3072]{1,0:T(8,128)(2,1)S(1)}, bf16[128,3072]{1,0:T(8,128)(2,1)}, u32[]{:S(2)}) copy-start(bf16[128,3072]{1,0:T(8,128)(2,1)} %shard_map.211) | copy-start | bytes 2359300
  213.5 8.2 %copy-start.19 = (bf16[128,3072]{1,0:T(8,128)(2,1)S(1)}, bf16[128,3072]{1,0:T(8,128)(2,1)}, u32[]{:S(2)}) copy-start(bf16[128,3072]{1,0:T(8,128)(2,1)} %shard_map.214) | copy-start | bytes 2359300
  216.0 44.1 %collective-permute-start.4 = (f32[1024,12]{1,0:T(8,128)}, f32[1024,12]{1,0:T(8,128)}, u32[]{:S(2)}, u32[]{:S(2)}) collective-permute-start(f32[1024,12]{1,0:T(8,128)} %bitcast.35), channel_id=1, source_target_pairs={{0,8},{8,0},{16,24},{24,16},{1,9},{9,1},{17,25},{25,17},{2,10},{10... | collective-permute-start | bytes 147464 | tf_op jit(solution)/shard_map/ppermute | solution.py:17
  232.5 35.7 %collective-permute-start.3 = (bf16[256,1536]{1,0:T(8,128)(2,1)}, bf16[256,1536]{1,0:T(8,128)(2,1)}, u32[]{:S(2)}, u32[]{:S(2)}) collective-permute-start(bf16[256,1536]{1,0:T(8,128)(2,1)} %bitcast.222), channel_id=1, source_target_pairs={{0,8},{8,0},{16,24},{24,16},{1,9},{9,1},{17,25},{25,17},{2,10},{10... | collective-permute-start | bytes 2359304 | tf_op jit(solution)/shard_map/ppermute | solution.py:17
  233.4 34.8 %collective-permute-start.2 = (bf16[256,1024]{1,0:T(8,128)(2,1)}, bf16[256,1024]{1,0:T(8,128)(2,1)}, u32[]{:S(2)}, u32[]{:S(2)}) collective-permute-start(bf16[256,1024]{1,0:T(8,128)(2,1)} %pad_maximum_fusion.5), channel_id=1, source_target_pairs={{0,8},{8,0},{16,24},{24,16},{1,9},{9,1},{17,25},{25,17},{2,10},{10... | collective-permute-start | bytes 1572872 | tf_op jit(solution)/shard_map/ppermute | solution.py:17
  234.7 28.2 %collective-permute-start = (bf16[256,1024]{1,0:T(8,128)(2,1)}, bf16[256,1024]{1,0:T(8,128)(2,1)}, u32[]{:S(2)}, u32[]{:S(2)}) collective-permute-start(bf16[256,1024]{1,0:T(8,128)(2,1)} %pad_maximum_fusion.3), channel_id=1, source_target_pairs={{0,8},{8,0},{16,24},{24,16},{1,9},{9,1},{17,25},{25,17},{2,10},{10... | collective-permute-start | bytes 1572872 | tf_op jit(solution)/shard_map/ppermute | solution.py:17
  237.8 25.1 %collective-permute-start.1 = (bf16[256,512]{1,0:T(8,128)(2,1)}, bf16[256,512]{1,0:T(8,128)(2,1)}, u32[]{:S(2)}, u32[]{:S(2)}) collective-permute-start(bf16[256,512]{1,0:T(8,128)(2,1)} %bitcast.224), channel_id=1, source_target_pairs={{0,8},{8,0},{16,24},{24,16},{1,9},{9,1},{17,25},{25,17},{2,10},{10... | collective-permute-start | bytes 786440 | tf_op jit(solution)/shard_map/ppermute | solution.py:17
  260.1 35.6 %collective-permute-start.12 = (bf16[256,2048]{1,0:T(8,128)(2,1)}, bf16[256,2048]{1,0:T(8,128)(2,1)}, u32[]{:S(2)}, u32[]{:S(2)}) collective-permute-start(bf16[256,2048]{1,0:T(8,128)(2,1)} %bitcast.257), channel_id=1, source_target_pairs={{0,8},{8,0},{16,24},{24,16},{1,9},{9,1},{17,25},{25,17},{2,10},{10... | collective-permute-start | bytes 3145736 | tf_op jit(solution)/shard_map/ppermute | solution.py:17
  262.9 32.8 %collective-permute-start.11 = (bf16[256,1024]{1,0:T(8,128)(2,1)}, bf16[256,1024]{1,0:T(8,128)(2,1)}, u32[]{:S(2)}, u32[]{:S(2)}) collective-permute-start(bf16[256,1024]{1,0:T(8,128)(2,1)} %pad_maximum_fusion.6), channel_id=1, source_target_pairs={{0,8},{8,0},{16,24},{24,16},{1,9},{9,1},{17,25},{25,17},{2,10},{10... | collective-permute-start | bytes 1572872 | tf_op jit(solution)/shard_map/ppermute | solution.py:17
  279.1 53.2 %collective-permute-start.5 = (bf16[2,2,128,2176]{2,3,1,0:T(8,128)(2,1)}, bf16[2,2,128,2176]{2,3,1,0:T(8,128)(2,1)}, u32[]{:S(2)}, u32[]{:S(2)}) collective-permute-start(bf16[2,2,128,2176]{2,3,1,0:T(8,128)(2,1)} %bitcast.250), channel_id=1, source_target_pairs={{0,2},{1,3},{2,0},{3,1},{4,6},{5,7},{6,4},{7,5},{8,10},{9,11},{10,... | collective-permute-start | bytes 6684680 | tf_op jit(solution)/shard_map/ppermute | solution.py:17
  290.9 13.6 %collective-permute-start.20 = (bf16[256,2048]{1,0:T(8,128)(2,1)}, bf16[256,2048]{1,0:T(8,128)(2,1)}, u32[]{:S(2)}, u32[]{:S(2)}) collective-permute-start(bf16[256,2048]{1,0:T(8,128)(2,1)} %bitcast.217), channel_id=1, source_target_pairs={{0,8},{8,0},{16,24},{24,16},{1,9},{9,1},{17,25},{25,17},{2,10},{10... | collective-permute-start | bytes 3145736 | tf_op jit(solution)/shard_map/ppermute | solution.py:17
  292.5 12.0 %collective-permute-start.19 = (bf16[256,1024]{1,0:T(8,128)(2,1)}, bf16[256,1024]{1,0:T(8,128)(2,1)}, u32[]{:S(2)}, u32[]{:S(2)}) collective-permute-start(bf16[256,1024]{1,0:T(8,128)(2,1)} %pad_maximum_fusion.7), channel_id=1, source_target_pairs={{0,8},{8,0},{16,24},{24,16},{1,9},{9,1},{17,25},{25,17},{2,10},{10... | collective-permute-start | bytes 1572872 | tf_op jit(solution)/shard_map/ppermute | solution.py:17
  295.7 15.4 %slice-start.2 = ((s8[6291456]{0:T(1024)(128)(4,1)}), s8[4194304]{0:T(1024)(128)(4,1)S(1)}, s32[]{:S(2)}) async-start(s8[6291456]{0:T(1024)(128)(4,1)} %bitcast.228), calls=%async_computation.2 | async-start | bytes 8388608
  302.2 48.0 %collective-permute-start.13 = (bf16[2,2,128,2048]{3,2,1,0:T(8,128)(2,1)}, bf16[2,2,128,2048]{3,2,1,0:T(8,128)(2,1)S(1)}, u32[]{:S(2)}, u32[]{:S(2)}) collective-permute-start(bf16[2,2,128,2048]{3,2,1,0:T(8,128)(2,1)} %dynamic-slice_bitcast_fusion.1), channel_id=1, source_target_pairs={{0,1},{1,0},{2,3},{3,2},{4,5},{5,4},{6,7},{7,6},{8,9},{9,8},{10,11... | collective-permute-start | bytes 6291464 | tf_op jit(solution)/shard_map/ppermute | solution.py:17
  311.1 84.2 %collective-permute-start.21 = (bf16[2,2,128,2048]{3,2,1,0:T(8,128)(2,1)}, bf16[2,2,128,2048]{3,2,1,0:T(8,128)(2,1)}, u32[]{:S(2)}, u32[]{:S(2)}) collective-permute-start(bf16[2,2,128,2048]{3,2,1,0:T(8,128)(2,1)} %dynamic-slice_bitcast_fusion), channel_id=1, source_target_pairs={{0,1},{1,0},{2,3},{3,2},{4,5},{5,4},{6,7},{7,6},{8,9},{9,8},{10,11... | collective-permute-start | bytes 6291464 | tf_op jit(solution)/shard_map/ppermute | solution.py:17
  332.3 17.9 %copy-start.28 = (bf16[1024,2048]{1,0:T(8,128)(2,1)S(1)}, bf16[1024,2048]{1,0:T(8,128)(2,1)}, u32[]{:S(2)}) copy-start(bf16[1024,2048]{1,0:T(8,128)(2,1)} %copy-done.27) | copy-start | bytes 12582916
  335.4 63.9 %collective-permute-start.6 = (bf16[2,128,2176]{1,2,0:T(8,128)(2,1)S(1)}, bf16[2,128,2176]{1,2,0:T(8,128)(2,1)S(1)}, u32[]{:S(2)}, u32[]{:S(2)}) collective-permute-start(bf16[2,128,2176]{1,2,0:T(8,128)(2,1)S(1)} %dynamic-slice_bitcast_fusion.2), channel_id=1, source_target_pairs={{0,4},{1,5},{2,6},{3,7},{4,0},{5,1},{6,2},{7,3},{8,12},{9,13},{10,... | collective-permute-start | bytes 3342344 | tf_op jit(solution)/shard_map/ppermute | solution.py:17
  350.2 45.0 %copy-start.30 = (bf16[1024,2048]{1,0:T(8,128)(2,1)S(1)}, bf16[1024,2048]{1,0:T(8,128)(2,1)}, u32[]{:S(2)}) copy-start(bf16[1024,2048]{1,0:T(8,128)(2,1)} %copy-done.29) | copy-start | bytes 12582916
  351.3 49.6 %collective-permute-start.14 = (bf16[2,2,64,2048]{3,2,1,0:T(8,128)(2,1)S(1)}, bf16[2,2,64,2048]{3,2,1,0:T(8,128)(2,1)S(1)}, u32[]{:S(2)}, u32[]{:S(2)}) collective-permute-start(bf16[2,2,64,2048]{3,2,1,0:T(8,128)(2,1)S(1)} %dynamic-slice_bitcast_fusion.3), channel_id=1, source_target_pairs={{0,16},{8,24},{16,0},{24,8},{1,17},{9,25},{17,1},{25,9},{2,18},{10... | collective-permute-start | bytes 3145736 | tf_op jit(solution)/shard_map/ppermute | solution.py:17
  398.0 23.7 %collective-permute-start.22 = (bf16[2,2,64,2048]{3,2,0,1:T(8,128)(2,1)S(1)}, bf16[2,2,64,2048]{3,2,0,1:T(8,128)(2,1)S(1)}, u32[]{:S(2)}, u32[]{:S(2)}) collective-permute-start(bf16[2,2,64,2048]{3,2,0,1:T(8,128)(2,1)S(1)} %bitcast.260), channel_id=1, source_target_pairs={{0,16},{8,24},{16,0},{24,8},{1,17},{9,25},{17,1},{25,9},{2,18},{10... | collective-permute-start | bytes 3145736 | tf_op jit(solution)/shard_map/ppermute | solution.py:17
  399.6 22.6 %collective-permute-start.7 = (bf16[128,2176]{0,1:T(8,128)(2,1)S(1)}, bf16[128,2176]{0,1:T(8,128)(2,1)S(1)}, u32[]{:S(2)}, u32[]{:S(2)}) collective-permute-start(bf16[128,2176]{0,1:T(8,128)(2,1)S(1)} %dynamic-slice_bitcast_fusion.4), channel_id=1, source_target_pairs={{0,1},{1,0},{2,3},{3,2},{4,5},{5,4},{6,7},{7,6},{8,9},{9,8},{10,11... | collective-permute-start | bytes 1671176 | tf_op jit(solution)/shard_map/ppermute | solution.py:17
  401.3 22.4 %collective-permute-start.15 = (bf16[2,64,2048]{2,1,0:T(8,128)(2,1)S(1)}, bf16[2,64,2048]{2,1,0:T(8,128)(2,1)S(1)}, u32[]{:S(2)}, u32[]{:S(2)}) collective-permute-start(bf16[2,64,2048]{2,1,0:T(8,128)(2,1)S(1)} %dynamic-slice_bitcast_fusion.6), channel_id=1, source_target_pairs={{0,2},{1,3},{2,0},{3,1},{4,6},{5,7},{6,4},{7,5},{8,10},{9,11},{10,... | collective-permute-start | bytes 1572872 | tf_op jit(solution)/shard_map/ppermute | solution.py:17
  422.1 17.1 %collective-permute-start.23 = (bf16[2,64,2048]{2,1,0:T(8,128)(2,1)S(1)}, bf16[2,64,2048]{2,1,0:T(8,128)(2,1)S(1)}, u32[]{:S(2)}, u32[]{:S(2)}) collective-permute-start(bf16[2,64,2048]{2,1,0:T(8,128)(2,1)S(1)} %dynamic-slice_bitcast_fusion.5), channel_id=1, source_target_pairs={{0,2},{1,3},{2,0},{3,1},{4,6},{5,7},{6,4},{7,5},{8,10},{9,11},{10,... | collective-permute-start | bytes 1572872 | tf_op jit(solution)/shard_map/ppermute | solution.py:17
  422.4 33.6 %collective-permute-start.8 = (bf16[128,2176]{0,1:T(8,128)(2,1)S(1)}, bf16[128,2176]{0,1:T(8,128)(2,1)S(1)}, u32[]{:S(2)}, u32[]{:S(2)}) collective-permute-start(bf16[128,2176]{0,1:T(8,128)(2,1)S(1)} %fusion.37), channel_id=1, source_target_pairs={{0,16},{8,24},{16,0},{24,8},{1,17},{9,25},{17,1},{25,9},{2,18},{10... | collective-permute-start | bytes 1671176 | tf_op jit(solution)/shard_map/ppermute | solution.py:17
  423.8 15.8 %collective-permute-start.16 = (bf16[64,2048]{1,0:T(8,128)(2,1)S(1)}, bf16[64,2048]{1,0:T(8,128)(2,1)S(1)}, u32[]{:S(2)}, u32[]{:S(2)}) collective-permute-start(bf16[64,2048]{1,0:T(8,128)(2,1)S(1)} %dynamic-slice_bitcast_fusion.8), channel_id=1, source_target_pairs={{0,4},{1,5},{2,6},{3,7},{4,0},{5,1},{6,2},{7,3},{8,12},{9,13},{10,... | collective-permute-start | bytes 786440 | tf_op jit(solution)/shard_map/ppermute | solution.py:17
  439.4 15.2 %collective-permute-start.24 = (bf16[64,2048]{1,0:T(8,128)(2,1)S(1)}, bf16[64,2048]{1,0:T(8,128)(2,1)S(1)}, u32[]{:S(2)}, u32[]{:S(2)}) collective-permute-start(bf16[64,2048]{1,0:T(8,128)(2,1)S(1)} %dynamic-slice_bitcast_fusion.7), channel_id=1, source_target_pairs={{0,4},{1,5},{2,6},{3,7},{4,0},{5,1},{6,2},{7,3},{8,12},{9,13},{10,... | collective-permute-start | bytes 786440 | tf_op jit(solution)/shard_map/ppermute | solution.py:17
  439.7 18.5 %collective-permute-start.17 = (bf16[64,2048]{1,0:T(8,128)(2,1)S(1)}, bf16[64,2048]{1,0:T(8,128)(2,1)S(1)}, u32[]{:S(2)}, u32[]{:S(2)}) collective-permute-start(bf16[64,2048]{1,0:T(8,128)(2,1)S(1)} %fusion.74), channel_id=1, source_target_pairs={{0,16},{8,24},{16,0},{24,8},{1,17},{9,25},{17,1},{25,9},{2,18},{10... | collective-permute-start | bytes 786440 | tf_op jit(solution)/shard_map/ppermute | solution.py:17
  454.7 7.4 %collective-permute-start.25 = (bf16[64,2048]{1,0:T(8,128)(2,1)S(1)}, bf16[64,2048]{1,0:T(8,128)(2,1)S(1)}, u32[]{:S(2)}, u32[]{:S(2)}) collective-permute-start(bf16[64,2048]{1,0:T(8,128)(2,1)S(1)} %fusion.73), channel_id=1, source_target_pairs={{0,16},{8,24},{16,0},{24,8},{1,17},{9,25},{17,1},{25,9},{2,18},{10... | collective-permute-start | bytes 786440 | tf_op jit(solution)/shard_map/ppermute | solution.py:17
  457.4 7.3 %collective-permute-start.9 = (bf16[128,1536]{0,1:T(8,128)(2,1)S(1)}, bf16[128,1536]{0,1:T(8,128)(2,1)S(1)}, u32[]{:S(2)}, u32[]{:S(2)}) collective-permute-start(bf16[128,1536]{0,1:T(8,128)(2,1)S(1)} %get-tuple-element.88), channel_id=1, source_target_pairs={{0,8},{8,0},{16,24},{24,16},{1,9},{9,1},{17,25},{25,17},{2,10},{10... | collective-permute-start | bytes 1179656 | tf_op jit(solution)/shard_map/ppermute | solution.py:17
  458.2 5.5 %collective-permute-start.10 = (bf16[128,512]{0,1:T(8,128)(2,1)S(1)}, bf16[128,512]{0,1:T(8,128)(2,1)S(1)}, u32[]{:S(2)}, u32[]{:S(2)}) collective-permute-start(bf16[128,512]{0,1:T(8,128)(2,1)S(1)} %get-tuple-element.86), channel_id=1, source_target_pairs={{0,8},{8,0},{16,24},{24,16},{1,9},{9,1},{17,25},{25,17},{2,10},{10... | collective-permute-start | bytes 393224 | tf_op jit(solution)/shard_map/ppermute | solution.py:17
  458.3 8.2 %collective-permute-start.18 = (bf16[128,2048]{1,0:T(8,128)(2,1)S(1)}, bf16[128,2048]{1,0:T(8,128)(2,1)}, u32[]{:S(2)}, u32[]{:S(2)}) collective-permute-start(bf16[128,2048]{1,0:T(8,128)(2,1)S(1)} %bitcast.255), channel_id=1, source_target_pairs={{0,8},{8,0},{16,24},{24,16},{1,9},{9,1},{17,25},{25,17},{2,10},{10... | collective-permute-start | bytes 1572872 | tf_op jit(solution)/shard_map/ppermute | solution.py:17
  462.3 10.3 %collective-permute-start.26 = (bf16[128,2048]{1,0:T(8,128)(2,1)S(1)}, bf16[128,2048]{1,0:T(8,128)(2,1)}, u32[]{:S(2)}, u32[]{:S(2)}) collective-permute-start(bf16[128,2048]{1,0:T(8,128)(2,1)S(1)} %bitcast.253), channel_id=1, source_target_pairs={{0,8},{8,0},{16,24},{24,16},{1,9},{9,1},{17,25},{25,17},{2,10},{10... | collective-permute-start | bytes 1572872 | tf_op jit(solution)/shard_map/ppermute | solution.py:17
  (58 other events, 172.3 us)

commit v2 on v1

--- a/solution.py
+++ b/solution.py
@@ -594,101 +594,248 @@
     return grad_hidden, vectors, pairs
 
 
-def swap(x, axis, bit):
-    return from_partner(x, axis, bit)
-
-
-def add_low(kept, received):
-    return (kept.astype(f32) + received.astype(f32)).astype(bf16)
-
-
-def pick(x, at, axis):
-    return lax.dynamic_index_in_dim(x, at, axis, keepdims=False)
-
-
-def fold(x, axis, index, mesh_axis, bit):
-    sent = pick(x, 1 - index, axis)
-    kept = pick(x, index, axis)
-    return add_low(kept, swap(sent, mesh_axis, bit))
-
-
-def join(x, index, mesh_axis, bit):
-    other = swap(x, mesh_axis, bit)
-    return jnp.where(index == 0, jnp.stack([x, other]), jnp.stack([other, x]))
-
-
-def reduce_yxz(total, position, row):
-    columns = total.shape[1]
-    z_hi, z_lo, y = position >> 2, position >> 1 & 1, position & 1
-    x_at = row >> 1
-    cut = total.reshape(2, 2, 2, 128, columns)
-    part = fold(cut, 2, y, "blk", 0)
-    part = part.reshape(2, 2, 2, 64, columns)
-    part = fold(part, 2, x_at, "batch", 1)
-    part = fold(part, 1, z_lo, "blk", 1)
-    part = fold(part, 0, z_hi, "blk", 2)
-    return join(part, x_at, "batch", 1).reshape(128, columns)
-
-
-def reduce_zyx(total, position, row):
-    columns = total.shape[1]
-    z_hi, z_lo, y = position >> 2, position >> 1 & 1, position & 1
-    cut = total.reshape(2, 2, 2, 128, columns)
-    part = fold(cut, 1, z_lo, "blk", 1)
-    part = fold(part, 0, z_hi, "blk", 2)
-    part = fold(part, 0, y, "blk", 0)
-    return add_low(part, swap(part, "batch", 1))
+PATHS = {"A": "yxabXC", "B": "xyabXC", "C": "abysC"}
+CHUNK_PATHS = "BCAACBBCABAA"
+WIDE = 512
+ORDER = (
+    (0, -1), (1, -1), (2, -1), (3, -1), (0, 0), (4, -1), (1, 0), (5, -1), (2, 0), (6, -1), (3, 0), (7, -1), (4, 0), (8, -1), (5, 0), (9, -1), (0, 1), (2, 1), (1, 1), (8, 0), (10, -1), (7, 0), (11, -1), (6, 0), (5, 1), (3, 1), (1, 2), (0, 2), (2, 2), (4, 1), (9, 0), (10, 0), (5, 2), (3, 2), (7, 1), (8, 1), (0, 3), (1, 3), (2, 3), (1, 4), (11, 0), (5, 3), (10, 1), (3, 3), (0, 4), (8, 2), (2, 4), (0, 5), (6, 1), (2, 5), (10, 2), (4, 2), (8, 3), (11, 1), (6, 2), (5, 4), (3, 4), (5, 5), (9, 1), (10, 3), (3, 5), (11, 2), (4, 3), (7, 2), (8, 4), (4, 4), (6, 3), (10, 4), (8, 5), (9, 2), (10, 5), (7, 3), (11, 3), (6, 4), (7, 4), (6, 5), (9, 3), (11, 4), (11, 5), (9, 4), (9, 5),
+)
+
+
+def plan(path, rows):
+    slabs, width, steps = 8, WIDE, []
+    for stage in path:
+        if stage in "yab":
+            slabs //= 2
+        elif stage == "x":
+            width //= 2
+        elif stage == "X":
+            width *= 2
+        steps.append((stage, slabs, width))
+    return steps
+
+
+def grad_kernel(*refs):
+    count = len(CHUNK_PATHS)
+    lefts, rights = refs[0:8], refs[8:16]
+    vec_ref, out = refs[16], refs[17]
+    it = iter(refs[18:])
+    left_buf = [next(it) for _ in range(4)]
+    right_buf = [next(it) for _ in range(4)]
+    turned = next(it)
+    chunk_buf = [next(it) for _ in range(count)]
+    landing = {}
+    for c, name in enumerate(CHUNK_PATHS):
+        for i, (stage, _, _) in enumerate(plan(PATHS[name], 128)):
+            if stage in "yabxs":
+                landing[c, i] = next(it)
+    send_sem, recv_sem, in_send, in_recv, in_own, vec_sem = it
+
+    row, position = lax.axis_index("batch"), lax.axis_index("blk")
+    core, x_at = row % 2, row // 2
+    y, z_lo, z_hi = position % 2, (position // 2) % 2, position // 4
+    bits = {"y": y, "a": z_lo, "b": z_hi}
+    across = {
+        "C": {"batch": row + 1 - 2 * core},
+        "x": {"batch": row + 2 - 4 * x_at},
+        "y": {"blk": position + 1 - 2 * y},
+        "a": {"blk": position + 2 - 4 * z_lo},
+        "b": {"blk": position + 4 - 8 * z_hi},
+    }
+    across["X"] = across["s"] = across["x"]
+    barrier = pltpu.get_barrier_semaphore()
+    for who in "Cxyab":
+        pl.semaphore_signal(barrier, inc=1, device_id=across[who], device_id_type=MESH)
+
+    order_of = (3, 2, 1, 0)
+    own_copies, in_copies = {}, {}
+    for k in order_of:
+        for d in range(2):
+            half = right_buf[k].shape[2]
+            mine = pl.ds(pl.multiple_of(core * half, 128), half)
+            for side, (src, dst) in enumerate(
+                ((lefts[2 * k + d], left_buf[k].at[d]), (rights[2 * k + d].at[:, mine], right_buf[k].at[d]))
+            ):
+                copy = pltpu.make_async_copy(src, dst, in_own.at[k, d, side])
+                copy.start()
+                own_copies[k, d, side] = copy
+    vec_c = count - 1
+    vec_copy = pltpu.make_async_copy(vec_ref, chunk_buf[vec_c].at[:, 128:144], vec_sem)
+    vec_copy.start()
+    pl.semaphore_wait(barrier, 5)
+    for k in order_of:
+        for d in range(2):
+            half = right_buf[k].shape[2]
+            theirs = pl.ds(pl.multiple_of((1 - core) * half, 128), half)
+            for side, (src, dst) in enumerate(
+                ((lefts[2 * k + d], left_buf[k].at[2 + d]), (rights[2 * k + d].at[:, theirs], right_buf[k].at[2 + d]))
+            ):
+                copy = pltpu.make_async_remote_copy(
+                    src_ref=src, dst_ref=dst, send_sem=in_send.at[k, d, side],
+                    recv_sem=in_recv.at[k, d, side], device_id=across["C"], device_id_type=MESH,
+                )
+                copy.start()
+                in_copies[k, d, side] = copy
+
+    def weight_of(c):
+        return (3, c, 2048) if c < 4 else (2, c - 4, 2048) if c < 8 else (1, 0, 512) if c < 9 else (0, c - 9, 1536)
+
+    base = {3: 0, 2: 4096, 1: 8192, 0: 9216}
+    ready = set()
+
+    def prepare(k):
+        for d in range(2):
+            for side in range(2):
+                own_copies[k, d, side].wait()
+                in_copies[k, d, side].wait_recv()
+        for g in range(4):
+            turned[:, pl.ds(128 * g, 128)] = left_buf[k][g].T
+
+    def compute(c):
+        k, at, _ = weight_of(c)
+        if k not in ready:
+            prepare(k)
+            ready.add(k)
+        path = [s for s in PATHS[CHUNK_PATHS[c]] if s in "yab"]
+        right = right_buf[k][:, :, pl.ds(at * WIDE, WIDE)].reshape(512, WIDE)
+
+        def piece(i, carry):
+            product = jnp.dot(
+                turned[pl.ds(pl.multiple_of(i * 256, 256), 256), :], right, preferred_element_type=f32
+            ).astype(bf16)
+            for low in range(2):
+                bit = {"y": low, "a": i % 2, "b": i // 2}
+                spot = (bit[path[0]] * 2 + bit[path[1]]) * 2 + bit[path[2]]
+                chunk_buf[c][spot, 0:128] = product[128 * low : 128 * low + 128]
+            return carry
+
+        lax.fori_loop(0, 4, piece, 0)
+        if c == vec_c:
+            vec_copy.wait()
+
+    current, copies = {}, {}
+    steps = {c: plan(PATHS[name], 128) for c, name in enumerate(CHUNK_PATHS)}
+    sem_at = {}
+    for c in range(count):
+        for i in range(len(steps[c])):
+            sem_at[c, i] = len(sem_at)
+
+    def spot_of(c):
+        k, at, half = weight_of(c)
+        return base[k] + core * half + at * WIDE
+
+    def rows_of(c):
+        return 144 if c == vec_c else 128
+
+    def send(c, i):
+        stage, slabs, width = steps[c][i]
+        if stage in "yab":
+            src = current[c].at[pl.ds((1 - bits[stage]) * slabs, slabs)]
+            dst = landing[c, i]
+        elif stage == "x":
+            src = current[c].at[:, :, pl.ds(pl.multiple_of((1 - x_at) * width, 128), width)]
+            dst = landing[c, i]
+        elif stage == "s":
+            src, dst = current[c], landing[c, i]
+        else:
+            start = spot_of(c) + (x_at * (width // 2) if stage == "X" else 0)
+            width = width // 2 if stage == "X" else width
+            src = dst = out.at[pl.ds(0, rows_of(c)), pl.ds(pl.multiple_of(start, 128), width)]
+        copy = pltpu.make_async_remote_copy(
+            src_ref=src, dst_ref=dst, send_sem=send_sem.at[sem_at[c, i]],
+            recv_sem=recv_sem.at[sem_at[c, i]], device_id=across[stage], device_id_type=MESH,
+        )
+        copy.start()
+        copies[c, i] = copy
+
+    def advance(c, i):
+        stage, slabs, width = steps[c][i]
+        copies[c, i].wait_recv()
+        if stage in "XC":
+            return
+        got, old = landing[c, i], current[c]
+
+        def add(n, carry):
+            if stage in "yab":
+                kept = old[bits[stage] * slabs + n]
+            elif stage == "x":
+                kept = old[n, :, pl.ds(pl.multiple_of(x_at * width, 128), width)]
+            else:
+                kept = old[n]
+            got[n] = (got[n].astype(f32) + kept.astype(f32)).astype(bf16)
+            return carry
+
+        lax.fori_loop(0, slabs, add, 0)
+        current[c] = got
+        if steps[c][i + 1][0] in "XC":
+            start = spot_of(c) + (x_at * width if steps[c][i + 1][0] == "X" else 0)
+            out[pl.ds(0, rows_of(c)), pl.ds(pl.multiple_of(start, 128), width)] = got[0]
+
+    for c, i in ORDER:
+        if i < 0:
+            compute(c)
+            current[c] = chunk_buf[c]
+        else:
+            advance(c, i)
+        if i + 1 < len(steps[c]):
+            send(c, i + 1)
+    for copy in copies.values():
+        copy.wait_send()
+    for copy in in_copies.values():
+        copy.wait_send()
+
+
+def weight_grads(pairs_two, pairs_one, vectors):
+    lefts, rights = [], []
+    for two, one in zip(pairs_two, pairs_one):
+        lefts += [two[0], one[0]]
+        rights += [two[1], one[1]]
+    scratch = [pltpu.VMEM((4, 128, 1024), bf16) for _ in range(4)]
+    scratch += [pltpu.VMEM((4, 128, rights[2 * k].shape[1] // 2), bf16) for k in range(4)]
+    scratch += [pltpu.VMEM((1024, 512), bf16)]
+    total = 0
+    rows = [144 if c == len(CHUNK_PATHS) - 1 else 128 for c in range(len(CHUNK_PATHS))]
+    scratch += [pltpu.VMEM((8, r, WIDE), bf16) for r in rows]
+    for c, name in enumerate(CHUNK_PATHS):
+        for stage, slabs, width in plan(PATHS[name], 128):
+            total += 1
+            if stage in "yabxs":
+                scratch.append(pltpu.VMEM((slabs, rows[c], width), bf16))
+    dma = pltpu.SemaphoreType.DMA
+    scratch += [dma((total,)), dma((total,)), dma((4, 2, 2)), dma((4, 2, 2)), dma((4, 2, 2)), dma(())]
+    return pl.pallas_call(
+        grad_kernel,
+        out_shape=jax.ShapeDtypeStruct((144, 12288), bf16),
+        in_specs=[pl.BlockSpec(memory_space=pl.ANY)] * 17,
+        out_specs=pl.BlockSpec(memory_space=pltpu.VMEM),
+        scratch_shapes=scratch,
+        compiler_params=pltpu.CompilerParams(
+            collective_id=5, has_side_effects=True, vmem_limit_bytes=56 * 2**20
+        ),
+    )(*lefts, *rights, vectors)
 
 
 def fast_body(tokens, lengths, *rest):
     params, cotangent = rest[:-1], rest[-1]
     group = lax.axis_size("blk")
-    position = lax.axis_index("blk")
-    row = lax.axis_index("batch")
-    core = row & 1
     out_one, saved_one = fast_forward(tokens[0].astype(f32), params, lengths, group)
     out_two, saved_two = fast_forward(out_one, params, lengths, group)
     grad, vec_two, pairs_two = fast_backward(cotangent[0].astype(f32), saved_two, params, lengths, group)
     grad, vec_one, pairs_one = fast_backward(grad, saved_one, params, lengths, group)
-
-    def half_grad(pair_two, pair_one):
-        def both(two, one, split):
-            mine = jnp.concatenate([two, one], 0)
-            if split:
-                halves = mine.reshape(mine.shape[0], 2, mine.shape[1] // 2)
-                mine, sent = pick(halves, core, 1), pick(halves, 1 - core, 1)
-            else:
-                sent = mine
-            return jnp.concatenate([mine, swap(sent, "batch", 0)], 0)
-
-        left = both(pair_two[0], pair_one[0], False)
-        right = both(pair_two[1], pair_one[1], True)
-        return dot_0(left, right).astype(bf16)
-
-    qkv_half, attn_half, in_half, back_half = [
-        half_grad(two, one) for two, one in zip(pairs_two, pairs_one)
-    ]
     vectors = [a + b for a, b in zip(vec_two, vec_one)]
     stacked = jnp.concatenate(
         [jnp.stack(vectors[:4] + vectors[5:]).reshape(8, 8, 128),
          vectors[4].reshape(8, 4, 128).transpose(1, 0, 2)], 0
     )
-    pieces = stacked.transpose(1, 2, 0).reshape(1024, 12)
-    pieces = pieces + swap(pieces, "batch", 0)
-    pieces = jnp.pad(pieces, ((0, 0), (0, 116))).astype(bf16)
-    back_part = reduce_yxz(back_half, position, row)
-    in_part = reduce_yxz(in_half, position, row)
-    tail = reduce_zyx(jnp.concatenate([attn_half, qkv_half, pieces], 1), position, row)
-
-    def whole(part):
-        both = join(part, core, "batch", 0)
-        return both.transpose(1, 0, 2).reshape(128, -1).astype(f32)
-
-    back_grad = whole(back_part).T
-    in_grad = whole(in_part)
-    attn_grad = whole(tail[:, :512])
-    qkv_grad = whole(tail[:, 512:2048])
-    small = tail[:, 2048:2060].astype(f32).T
+    pieces = stacked.reshape(3, 4, 2, 2, 2, 128).transpose(4, 3, 2, 0, 1, 5).reshape(8, 3, 512)
+    pieces = jnp.pad(pieces, ((0, 0), (0, 13), (0, 0))).astype(bf16)
+    sums = weight_grads(pairs_two, pairs_one, pieces)
+    back_grad = sums[:128, :4096].astype(f32).T
+    in_grad = sums[:128, 4096:8192].astype(f32)
+    attn_grad = sums[:128, 8192:9216].astype(f32)
+    qkv_grad = sums[:128, 9216:].astype(f32)
+    small = sums[128:131, 10240:10752].astype(f32) + sums[128:131, 11776:12288].astype(f32)
+    small = small.reshape(12, 128)
     return (
         out_two.astype(bf16)[None],
         grad.astype(bf16)[None],

time: 485 us -> 366 us (0.75)
  Pallas kernels: 131 us -> 258 us
  waiting for transfers between devices: 119 us -> 0 us
  local copies, waits for them, and re-layouts: 85.6 us -> 17.1 us
  starting transfers between devices: 30.5 us -> 0 us
  other arithmetic: 30.4 us -> 15.5 us
  matrix products: 78.4 us -> 66.5 us
    pallas_call x0 -> x1, Pallas kernels: none -> 127 us  [weight_grads(): pl.pallas_call(grad_kernel, out_shape=jax.ShapeDtypeStruct((144, 12288),...]
    ppermute x27 -> x0, waiting for transfers between devices: 119 us -> none  [from_partner(): lax.ppermute(x, axis, [(i, i ^ 1 << distance) for i in range(lax.axis_siz...]
    ppermute x27 -> x0, starting transfers between devices: 30.5 us -> none  [from_partner(): lax.ppermute(x, axis, [(i, i ^ 1 << distance) for i in range(lax.axis_siz...]
    dynamic_slice x8 -> x0, local copies, waits for them, and re-layouts: 25.4 us -> none  [pick(): return lax.dynamic_index_in_dim(x, at, axis, keepdims=False)]
    unnamed x170 -> x101, local copies, waits for them, and re-layouts: 34.5 us -> 14.2 us
    dot_general x4 -> x0, matrix products: 14.4 us -> none  [dot_0(): lax.dot_general(a, b, (((0,), (0,)), ((), ())), preferred_element_type=f32)]
    reshape x5 -> x3, local copies, waits for them, and re-layouts: 11.8 us -> 0.04 us  [the longest x2 0.03 us: fast_body(): stacked.reshape(3, 4, 2, 2, 2, 128).transpose(4, 3, 2, 0, 1, 5)]
    concatenate x9 -> x0, other arithmetic: 8.11 us -> none  [the longest x8 7.76 us: both(): mine = jnp.concatenate([two, one], 0)]
  transfers between devices with their start and end apart: 27 -> 0, of which waited for: 7 -> 0; matrix products, arithmetic and copies ran while one was open for 22% -> 0% of each run, Pallas kernels for 0% -> 0%
where the time goes in v2:
time: 366 us; the launch traced here: 360 us
  Pallas kernels  258 us (70%)
  matrix products  66.5 us (18%)
  local copies, waits for them, and re-layouts  17.1 us (5%)
  other arithmetic  15.5 us (4%)
    pallas_call x1, Pallas kernels, weight_grads(): pl.pallas_call(grad_kernel, out_shape=jax.ShapeDtypeStruct((144, 12288),...  127 us
    pallas_call x8, Pallas kernels, exchange(): pl.pallas_call(functools.partial(exchange_kernel, group, groups * 128, sp...  105 us
    dot_general x8, matrix products, dot_t(): lax.dot_general(a, b, (((1,), (1,)), ((), ())), preferred_element_type=f32)  33.5 us
    dot_general x2, matrix products, fast_forward(): inner_pre = jnp.dot(first_low, w_in, preferred_element_type=f32) + in_bias  19.9 us
    pallas_call x2, Pallas kernels, attend_back(): pl.pallas_call(attend_back_kernel, out_shape=jax.ShapeDtypeStruct((count,...  16 us
    unnamed x101, local copies, waits for them, and re-layouts  14.2 us
    pallas_call x2, Pallas kernels, attend(): pl.pallas_call(attend_kernel, out_shape=(jax.ShapeDtypeStruct((count, 128...  10.4 us

profile of v2, /device:TPU:1, one launch (start us, length us, event | category | flops | bytes accessed | tf_op | source)
XLA Modules:
  0.0 359.7 jit_solution(2049659643263117733)
XLA Ops:
  0.7 0.9 fusion.52
  1.6 4.8 %fusion.src = bf16[128,3072]{1,0:T(8,128)(2,1)} fusion(bf16[1024,3072]{1,0:T(8,128)(2,1)} %param.14, f32[3072]{0:T(1024)S(1)} %pad_maximum_fusion, bf16[1,128,1024]{2,1,0:T(8,128)(2,1)} %param.12), kind=kOutput, calls=%fused_computation.4 | convolution fusion | flops 806092800 | bytes 7352320 | tf_op jit(solution)/shard_map/dot_general | solution.py:538
  6.3 17.9 %shard_map.203.qkv_ref = bf16[1024,384]{1,0:T(8,128)(2,1)} custom-call(bf16[128,3072]{1,0:T(8,128)(2,1)} %fusion.src), custom_call_target="tpu_custom_call" | custom-call | tf_op jit(solution)/shard_map/pallas_call | solution.py:408
  24.9 1.1 copy-done.1
  26.0 5.2 %shard_map.204 = (bf16[1024,128]{1,0:T(8,128)(2,1)S(1)}, f32[1024,128]{1,0:T(8,128)S(1)}) custom-call(s32[1]{0:T(128)S(6)} %copy.53.len_ref, bf16[1024,384]{1,0:T(8,128)(2,1)S(1)} %copy-done.1), custom_call_target="tpu_custom_call" | custom-call | flops 536870912 | bytes 2097152 | tf_op jit(solution)/shard_map/pallas_call | solution.py:458
  31.2 0.7 copy-done.9
  31.9 11.4 %shard_map.205.refs_3_ = bf16[128,1024]{1,0:T(8,128)(2,1)} custom-call(bf16[1024,128]{1,0:T(8,128)(2,1)} %copy-done.9), custom_call_target="tpu_custom_call" | custom-call | tf_op jit(solution)/shard_map/pallas_call | solution.py:408
  43.4 1.5 fusion.53
  45.3 10.1 %multiply_convert_fusion.1 = (bf16[128,4096]{1,0:T(8,128)(2,1)S(1)}, f32[128,4096]{1,0:T(8,128)}, f32[128,4096]{1,0:T(8,128)}) fusion(f32[4096]{0:T(1024)S(1)} %copy-done.37, bf16[128,1024]{1,0:T(8,128)(2,1)S(1)} %fusion.29.refs_5_, bf16[1024,4096]{1,0:T(8,128)(2,1)} %param.18), kind=kOutput, calls=%fused_computation.28 | convolution fusion | flops 1108344832 | bytes 13910016 | tf_op jit(solution)/shard_map/dot_general | solution.py:545
  55.5 1.5 fusion.54
  58.0 0.7 copy-done.25
  58.8 1.9 fusion.1.src
  60.7 14.9 %shard_map.206.qkv_ref = bf16[1024,384]{1,0:T(8,128)(2,1)} custom-call(bf16[128,3072]{1,0:T(8,128)(2,1)} %fusion.1.src), custom_call_target="tpu_custom_call" | custom-call | tf_op jit(solution)/shard_map/pallas_call | solution.py:408
  75.7 1.1 copy-done.3
  76.8 5.2 %shard_map.207 = (bf16[1024,128]{1,0:T(8,128)(2,1)S(1)}, f32[1024,128]{1,0:T(8,128)S(1)}) custom-call(s32[1]{0:T(128)S(6)} %copy.53.len_ref, bf16[1024,384]{1,0:T(8,128)(2,1)S(1)} %copy-done.3), custom_call_target="tpu_custom_call" | custom-call | flops 536870912 | bytes 2097152 | tf_op jit(solution)/shard_map/pallas_call | solution.py:458
  82.7 13.5 %shard_map.208.refs_2_ = bf16[128,1024]{1,0:T(8,128)(2,1)} custom-call(bf16[1024,128]{1,0:T(8,128)(2,1)} %copy-done.10), custom_call_target="tpu_custom_call" | custom-call | tf_op jit(solution)/shard_map/pallas_call | solution.py:408
  96.2 1.9 fusion.55
  98.5 9.8 %multiply_convert_fusion = (bf16[128,4096]{1,0:T(8,128)(2,1)S(1)}, f32[128,4096]{1,0:T(8,128)}, f32[128,4096]{1,0:T(8,128)}) fusion(f32[4096]{0:T(1024)S(1)} %copy-done.37, bf16[128,1024]{1,0:T(8,128)(2,1)S(1)} %fusion.31.refs_4_, bf16[1024,4096]{1,0:T(8,128)(2,1)} %param.18), kind=kOutput, calls=%fused_computation.15 | convolution fusion | flops 1108344832 | bytes 13910016 | tf_op jit(solution)/shard_map/dot_general | solution.py:545
  108.4 1.5 fusion.56
  110.5 1.0 convert_reduce_fusion.6
  111.4 5.8 %convert_reduce_fusion.1 = (f32[4096]{0:T(1024)S(1)}, bf16[128,4096]{1,0:T(8,128)(2,1)S(1)}) fusion(f32[128,4096]{1,0:T(8,128)} %get-tuple-element.94, f32[128,4096]{1,0:T(8,128)} %get-tuple-element.121, bf16[128,1024]{1,0:T(8,128)(2,1)S(1)} %get-tuple-element.86.refs_6_, bf16[4096,1024]{1,0:T(8,128)(2,1)S(1)} %bitcast.102), kind=kOutput, calls=%fused_computation.12 | convolution fusion | flops 1082126336 | bytes 13910016 | tf_op jit(solution)/shard_map/dot_general | solution.py:423
  117.3 3.1 multiply_reduce_fusion.2
  120.4 1.0 convert_reduce_fusion.8
  122.1 1.5 convolution_convert_fusion.1.src
  123.7 7.3 %shard_map.209.do_ref = bf16[1024,128]{1,0:T(8,128)(2,1)} custom-call(bf16[128,1024]{1,0:T(8,128)(2,1)} %convolution_convert_fusion.1.src), custom_call_target="tpu_custom_call" | custom-call | tf_op jit(solution)/shard_map/pallas_call | solution.py:408
  131.0 0.9 copy-done.8
  131.9 1.0 copy-done.12
  133.0 8.0 %shard_map.210.src = bf16[1024,384]{1,0:T(8,128)(2,1)S(1)} custom-call(s32[1]{0:T(128)S(6)} %copy.53.len_ref, bf16[1024,384]{1,0:T(8,128)(2,1)S(1)} %copy-done.4, bf16[1024,128]{1,0:T(8,128)(2,1)S(1)} %copy-done.8, f32[1024,128]{1,0:T(8,128)S(1)} %copy-done.12), custom_call_target="tpu_custom_call" | custom-call | flops 1342177280 | bytes 3145728 | tf_op jit(solution)/shard_map/pallas_call | solution.py:520
  141.0 0.9 copy-done.6
  141.8 12.8 %shard_map.211.refs_8_ = bf16[128,3072]{1,0:T(8,128)(2,1)} custom-call(bf16[1024,384]{1,0:T(8,128)(2,1)} %copy-done.6), custom_call_target="tpu_custom_call" | custom-call | tf_op jit(solution)/shard_map/pallas_call | solution.py:408
  154.7 5.8 %multiply_reduce_fusion = (f32[1024]{0:T(1024)S(1)}, f32[128]{0:T(128)S(1)}, f32[128]{0:T(128)S(1)}, f32[1024]{0:T(1024)S(1)}, f32[128,1024]{1,0:T(8,128)S(1)}) fusion(f32[128,1024]{1,0:T(8,128)} %copy-done.15, f32[128]{0:T(128)S(1)} %add_rsqrt_fusion.2, f32[128]{0:T(128)S(1)} %broadcast_multiply_fusion.10, f32[1024]{0:T(1024)S(1)} %bitcast.121, ...), kind=kOutput, calls=%fused_computation.74 | convolution fusion | flops 806614784 | bytes 8665088 | tf_op jit(solution)/shard_map/dot_general | solution.py:423
  160.8 7.0 %convert_reduce_fusion = (f32[4096]{0:T(1024)S(1)}, bf16[128,4096]{1,0:T(8,128)(2,1)S(1)}) fusion(f32[128,4096]{1,0:T(8,128)S(1)} %copy-done.38, f32[128,4096]{1,0:T(8,128)S(1)} %copy-done.39, bf16[128,1024]{1,0:T(8,128)(2,1)S(1)} %get-tuple-element.83.refs_7_, bf16[4096,1024]{1,0:T(8,128)(2,1)} %param.20), kind=kOutput, calls=%fused_computation.11 | convolution fusion | flops 1082126336 | bytes 13910016 | tf_op jit(solution)/shard_map/dot_general | solution.py:423
  167.9 3.1 multiply_reduce_fusion.1
  171.1 1.0 convert_reduce_fusion.7
  172.9 1.5 convolution_convert_fusion.src
  174.4 14.3 %shard_map.212.do_ref = bf16[1024,128]{1,0:T(8,128)(2,1)} custom-call(bf16[128,1024]{1,0:T(8,128)(2,1)} %convolution_convert_fusion.src), custom_call_target="tpu_custom_call" | custom-call | tf_op jit(solution)/shard_map/pallas_call | solution.py:408
  188.7 0.9 copy-done.7
  189.7 8.0 %shard_map.213.src = bf16[1024,384]{1,0:T(8,128)(2,1)S(1)} custom-call(s32[1]{0:T(128)S(6)} %copy.53.len_ref, bf16[1024,384]{1,0:T(8,128)(2,1)S(1)} %copy-done.2, bf16[1024,128]{1,0:T(8,128)(2,1)S(1)} %copy-done.7, f32[1024,128]{1,0:T(8,128)S(1)} %get-tuple-element.18.lse_ref), custom_call_target="tpu_custom_call" | custom-call | flops 1342177280 | bytes 3145728 | tf_op jit(solution)/shard_map/pallas_call | solution.py:520
  197.7 0.9 copy-done.5
  198.6 12.5 %shard_map.214.refs_9_ = bf16[128,3072]{1,0:T(8,128)(2,1)} custom-call(bf16[1024,384]{1,0:T(8,128)(2,1)} %copy-done.5), custom_call_target="tpu_custom_call" | custom-call | tf_op jit(solution)/shard_map/pallas_call | solution.py:408
  211.0 1.3 convert_reduce_fusion.2
  213.4 127.2 %shard_map.215 = bf16[144,12288]{1,0:T(8,128)(2,1)} custom-call(bf16[128,1024]{1,0:T(8,128)(2,1)} %copy-done.25, bf16[128,1024]{1,0:T(8,128)(2,1)} %bitcast.107, bf16[128,1024]{1,0:T(8,128)(2,1)} %shard_map.208.refs_2_, bf16[128,1024]{1,0:T(8,128)(2,1)} %shard_map.205.refs_3_, bf16[128,1024]{1,0:T(8,128)(2,1)} %copy-done.31, bf16[128,1024]{1,0:T(8,128)(2,1)} %copy-done.30, ...), custom_call_target="tpu_custom_call" | custom-call | tf_op jit(solution)/shard_map/pallas_call | solution.py:806
  340.6 4.0 %convert_bitcast_fusion = (f32[4096,128]{0,1:T(8,128)}, f32[128,4096]{1,0:T(8,128)}) fusion(bf16[144,12288]{1,0:T(8,128)(2,1)} %shard_map.215), kind=kLoop, calls=%fused_computation.10 | loop fusion | flops 1048576 | bytes 6291456 | tf_op jit(solution)/shard_map/transpose | solution.py:833
  344.7 2.9 copy.50
  347.6 2.5 slice_convert_fusion.1
  350.1 1.8 slice_convert_fusion.2
  351.9 0.7 convert_add_fusion
  353.8 5.7 %fusion.19 = bf16[1,128,1024]{2,1,0:T(8,128)(2,1)} fusion(f32[128,1024]{1,0:T(8,128)S(1)} %copy-done.29, bf16[128,3072]{1,0:T(8,128)(2,1)S(1)} %copy-done.18, bf16[1024,3072]{1,0:T(8,128)(2,1)} %param.14), kind=kOutput, calls=%fused_computation.60 | convolution fusion | flops 805568512 | bytes 7864320 | tf_op jit(solution)/shard_map/dot_general | solution.py:423
  (151 shorter events, 7.1 us)
Async XLA Ops:
  0.6 42.7 %copy-start = (bf16[1024,1024]{1,0:T(8,128)(2,1)S(1)}, bf16[1024,1024]{1,0:T(8,128)(2,1)}, u32[]{:S(2)}) copy-start(bf16[1024,1024]{1,0:T(8,128)(2,1)} %param.16) | copy-start | bytes 6291460
  24.8 1.1 copy-start.1
  26.0 17.3 %copy-start.34 = (f32[2,1024]{1,0:T(2,128)S(1)}, f32[2,1024]{1,0:T(2,128)}, u32[]{:S(2)}) copy-start(f32[2,1024]{1,0:T(2,128)} %param.17) | copy-start | bytes 24580
  26.0 17.4 %copy-start.26 = (bf16[1,128,1024]{2,1,0:T(8,128)(2,1)S(1)}, bf16[1,128,1024]{2,1,0:T(8,128)(2,1)}, u32[]{:S(2)}) copy-start(bf16[1,128,1024]{2,1,0:T(8,128)(2,1)} %param.12) | copy-start | bytes 786436
  31.2 0.7 copy-start.9
  31.9 13.2 %copy-start.35 = (f32[2,1024]{1,0:T(2,128)S(1)}, f32[2,1024]{1,0:T(2,128)}, u32[]{:S(2)}) copy-start(f32[2,1024]{1,0:T(2,128)} %param.21) | copy-start | bytes 24580
  31.9 13.2 %copy-start.36 = (f32[2,1024]{1,0:T(2,128)S(1)}, f32[2,1024]{1,0:T(2,128)}, u32[]{:S(2)}) copy-start(f32[2,1024]{1,0:T(2,128)} %param.22) | copy-start | bytes 24580
  43.3 2.0 copy-start.37
  44.8 10.6 %copy-start.13 = (f32[128,1024]{1,0:T(8,128)}, f32[128,1024]{1,0:T(8,128)S(1)}, u32[]{:S(2)}) copy-start(f32[128,1024]{1,0:T(8,128)S(1)} %get-tuple-element.115) | copy-start | bytes 1572868
  44.9 10.6 %slice-start.2 = ((s8[8388608]{0:T(1024)(128)(4,1)}), s8[4194304]{0:T(1024)(128)(4,1)S(1)}, s32[]{:S(2)}) async-start(s8[8388608]{0:T(1024)(128)(4,1)} %bitcast.99), calls=%async_computation.2 | async-start | bytes 8388608
  45.3 10.1 %copy-start.30 = (bf16[128,1024]{1,0:T(8,128)(2,1)}, bf16[128,1024]{1,0:T(8,128)(2,1)S(1)}, u32[]{:S(2)}) copy-start(bf16[128,1024]{1,0:T(8,128)(2,1)S(1)} %fusion.29.refs_5_) | copy-start | bytes 786436
  45.3 10.1 %slice-start.3 = ((s8[8388608]{0:T(1024)(128)(4,1)}), s8[4194304]{0:T(1024)(128)(4,1)S(1)}, s32[]{:S(2)}) async-start(s8[8388608]{0:T(1024)(128)(4,1)} %bitcast.99), calls=%async_computation.3 | async-start | bytes 8388608
  55.4 1.6 copy-start.19
  55.4 3.2 slice-start
  55.5 3.4 slice-start.1
  57.0 0.8 copy-start.15
  57.9 0.7 copy-start.25
  75.7 1.1 copy-start.3
  82.0 0.7 copy-start.10
  82.7 15.6 %copy-start.11 = (f32[1024,128]{1,0:T(8,128)}, f32[1024,128]{1,0:T(8,128)S(1)}, u32[]{:S(2)}) copy-start(f32[1024,128]{1,0:T(8,128)S(1)} %get-tuple-element.17.lse_ref) | copy-start | bytes 1572868
  96.2 12.2 %slice-start.4 = ((s8[8388608]{0:T(1024)(128)(4,1)}), s8[4194304]{0:T(1024)(128)(4,1)S(1)}, s32[]{:S(2)}) async-start(s8[8388608]{0:T(1024)(128)(4,1)} %bitcast.101), calls=%async_computation.4 | async-start | bytes 8388608
  98.5 9.9 %copy-start.31 = (bf16[128,1024]{1,0:T(8,128)(2,1)}, bf16[128,1024]{1,0:T(8,128)(2,1)S(1)}, u32[]{:S(2)}) copy-start(bf16[128,1024]{1,0:T(8,128)(2,1)S(1)} %fusion.31.refs_4_) | copy-start | bytes 786436
  98.5 9.9 %slice-start.5 = ((s8[8388608]{0:T(1024)(128)(4,1)}), s8[4194304]{0:T(1024)(128)(4,1)S(1)}, s32[]{:S(2)}) async-start(s8[8388608]{0:T(1024)(128)(4,1)} %bitcast.101), calls=%async_computation.5 | async-start | bytes 8388608
  108.4 1.6 copy-start.20
  108.4 1.8 copy-start.23
  109.9 7.3 %slice-start.6 = ((s8[8388608]{0:T(1024)(128)(4,1)}), s8[4194304]{0:T(1024)(128)(4,1)S(1)}, s32[]{:S(2)}) async-start(s8[8388608]{0:T(1024)(128)(4,1)} %bitcast.103), calls=%async_computation.6 | async-start | bytes 8388608
  111.4 5.8 %copy-start.32 = (bf16[128,1024]{1,0:T(8,128)(2,1)}, bf16[128,1024]{1,0:T(8,128)(2,1)S(1)}, u32[]{:S(2)}) copy-start(bf16[128,1024]{1,0:T(8,128)(2,1)S(1)} %get-tuple-element.86.refs_6_) | copy-start | bytes 786436
  111.4 5.8 %slice-start.7 = ((s8[8388608]{0:T(1024)(128)(4,1)}), s8[4194304]{0:T(1024)(128)(4,1)S(1)}, s32[]{:S(2)}) async-start(s8[8388608]{0:T(1024)(128)(4,1)} %bitcast.103), calls=%async_computation.7 | async-start | bytes 8388608
  117.2 3.2 copy-start.21
  120.4 10.5 %copy-start.4 = (bf16[1024,384]{1,0:T(8,128)(2,1)S(1)}, bf16[1024,384]{1,0:T(8,128)(2,1)}, u32[]{:S(2)}) copy-start(bf16[1024,384]{1,0:T(8,128)(2,1)} %shard_map.206.qkv_ref) | copy-start | bytes 2359300
  131.0 1.0 copy-start.8
  131.9 1.0 copy-start.12
  141.0 0.9 copy-start.6
  154.7 5.8 %copy-start.16 = (f32[128,1024]{1,0:T(8,128)S(1)}, f32[128,1024]{1,0:T(8,128)}, u32[]{:S(2)}) copy-start(f32[128,1024]{1,0:T(8,128)} %copy-done.15) | copy-start | bytes 1572868
  154.7 6.1 %copy-start.38 = (f32[128,4096]{1,0:T(8,128)S(1)}, f32[128,4096]{1,0:T(8,128)}, u32[]{:S(2)}) copy-start(f32[128,4096]{1,0:T(8,128)} %get-tuple-element.96) | copy-start | bytes 6291460
  154.7 6.1 %copy-start.39 = (f32[128,4096]{1,0:T(8,128)S(1)}, f32[128,4096]{1,0:T(8,128)}, u32[]{:S(2)}) copy-start(f32[128,4096]{1,0:T(8,128)} %get-tuple-element.116) | copy-start | bytes 6291460
  154.7 13.2 %slice-start.8 = ((s8[8388608]{0:T(1024)(128)(4,1)}), s8[4194304]{0:T(1024)(128)(4,1)S(1)}, s32[]{:S(2)}) async-start(s8[8388608]{0:T(1024)(128)(4,1)} %bitcast.105), calls=%async_computation.8 | async-start | bytes 8388608
  160.8 7.1 %copy-start.33 = (bf16[128,1024]{1,0:T(8,128)(2,1)}, bf16[128,1024]{1,0:T(8,128)(2,1)S(1)}, u32[]{:S(2)}) copy-start(bf16[128,1024]{1,0:T(8,128)(2,1)S(1)} %get-tuple-element.83.refs_7_) | copy-start | bytes 786436
  160.8 7.1 %slice-start.9 = ((s8[8388608]{0:T(1024)(128)(4,1)}), s8[4194304]{0:T(1024)(128)(4,1)S(1)}, s32[]{:S(2)}) async-start(s8[8388608]{0:T(1024)(128)(4,1)} %bitcast.105), calls=%async_computation.9 | async-start | bytes 8388608
  160.8 7.1 %copy-start.14 = (f32[128,1024]{1,0:T(8,128)S(1)}, f32[128,1024]{1,0:T(8,128)}, u32[]{:S(2)}) copy-start(f32[128,1024]{1,0:T(8,128)} %copy-done.13) | copy-start | bytes 1572868
  167.8 3.1 copy-start.22
  171.1 17.6 %copy-start.2 = (bf16[1024,384]{1,0:T(8,128)(2,1)S(1)}, bf16[1024,384]{1,0:T(8,128)(2,1)}, u32[]{:S(2)}) copy-start(bf16[1024,384]{1,0:T(8,128)(2,1)} %shard_map.203.qkv_ref) | copy-start | bytes 2359300
  188.7 1.0 copy-start.7
  197.7 0.9 copy-start.5
  198.6 13.7 %copy-start.17 = (bf16[128,3072]{1,0:T(8,128)(2,1)S(1)}, bf16[128,3072]{1,0:T(8,128)(2,1)}, u32[]{:S(2)}) copy-start(bf16[128,3072]{1,0:T(8,128)(2,1)} %shard_map.211.refs_8_) | copy-start | bytes 2359300
  198.6 13.9 %copy-start.24 = (bf16[1,128,1024]{2,1,0:T(8,128)(2,1)S(1)}, bf16[1,128,1024]{2,1,0:T(8,128)(2,1)}, u32[]{:S(2)}) copy-start(bf16[1,128,1024]{2,1,0:T(8,128)(2,1)} %param.23) | copy-start | bytes 786436
  347.6 6.2 %copy-start.18 = (bf16[128,3072]{1,0:T(8,128)(2,1)S(1)}, bf16[128,3072]{1,0:T(8,128)(2,1)}, u32[]{:S(2)}) copy-start(bf16[128,3072]{1,0:T(8,128)(2,1)} %shard_map.214.refs_9_) | copy-start | bytes 2359300
  347.6 6.2 %copy-start.29 = (f32[128,1024]{1,0:T(8,128)S(1)}, f32[128,1024]{1,0:T(8,128)}, u32[]{:S(2)}) copy-start(f32[128,1024]{1,0:T(8,128)} %get-tuple-element.89) | copy-start | bytes 1572868
  (2 other events, 1.4 us)
